TPU v7x, 32 devices: a whole 2x2x4 slice. The times are simulated.
32 devices in a mesh: dp: 16 (over z, y, core), tensor: 2 (over x).
Axes of the slice: x: 2, y: 2, z: 4, core: 2. Of those that a mesh axis runs over, the one named last changes fastest.
Arguments:
- inputs: bfloat16 [16384, 768], P(('dp', 'tensor')), may hold values from -6 to 6
- lengths: int32 [32], P('dp'), may hold values from 128 to 512, as said below
- teacher_query_weight: bfloat16 [768, 768], P('dp', 'tensor'), may hold values from -0.21875 to 0.21875
- teacher_query_bias: bfloat16 [2, 384], P('tensor', 'dp'), may hold values from -3 to 3
- teacher_key_weight: bfloat16 [768, 768], P('dp', 'tensor'), may hold values from -0.21875 to 0.21875
- teacher_value_weight: bfloat16 [768, 768], P('dp', 'tensor'), may hold values from -0.21875 to 0.21875
- teacher_value_bias: bfloat16 [2, 384], P('tensor', 'dp'), may hold values from -0.29882812 to 0.29882812
- teacher_output_weight: bfloat16 [768, 768], P('tensor', 'dp'), may hold values from -2.5 to 2.5
- teacher_output_bias: float32 [768], P(('dp', 'tensor')), may hold values from -3 to 3
- teacher_first_gain: float32 [768], P(('dp', 'tensor')), may hold values from 0.1 to 1.9
- teacher_first_shift: float32 [768], P(('dp', 'tensor')), may hold values from -3 to 3
- teacher_up_weight: bfloat16 [768, 3072], P('dp', 'tensor'), may hold values from -0.21875 to 0.21875
- teacher_up_bias: bfloat16 [2, 1536], P('tensor', 'dp'), may hold values from -3 to 3
- teacher_down_weight: bfloat16 [3072, 768], P('tensor', 'dp'), may hold values from -0.109375 to 0.109375
- teacher_down_bias: float32 [768], P(('dp', 'tensor')), may hold values from -3 to 3
- teacher_second_gain: float32 [768], P(('dp', 'tensor')), may hold values from 0.1 to 1.9
- teacher_second_shift: float32 [768], P(('dp', 'tensor')), may hold values from -3 to 3
- student_query_weight: bfloat16 [768, 768], P('dp', 'tensor'), may hold values from -0.21875 to 0.21875
- student_query_bias: bfloat16 [2, 384], P('tensor', 'dp'), may hold values from -3 to 3
- student_key_weight: bfloat16 [768, 768], P('dp', 'tensor'), may hold values from -0.21875 to 0.21875
- student_value_weight: bfloat16 [768, 768], P('dp', 'tensor'), may hold values from -0.21875 to 0.21875
- student_value_bias: bfloat16 [2, 384], P('tensor', 'dp'), may hold values from -0.29882812 to 0.29882812
- student_output_weight: bfloat16 [768, 768], P('tensor', 'dp'), may hold values from -2.5 to 2.5
- student_output_bias: float32 [768], P(('dp', 'tensor')), may hold values from -3 to 3
- student_first_gain: float32 [768], P(('dp', 'tensor')), may hold values from 0.1 to 1.9
- student_first_shift: float32 [768], P(('dp', 'tensor')), may hold values from -3 to 3
- student_up_weight: bfloat16 [768, 3072], P('dp', 'tensor'), may hold values from -0.21875 to 0.21875
- student_up_bias: bfloat16 [2, 1536], P('tensor', 'dp'), may hold values from -3 to 3
- student_down_weight: bfloat16 [3072, 768], P('tensor', 'dp'), may hold values from -0.109375 to 0.109375
- student_down_bias: float32 [768], P(('dp', 'tensor')), may hold values from -3 to 3
- student_second_gain: float32 [768], P(('dp', 'tensor')), may hold values from 0.1 to 1.9
- student_second_shift: float32 [768], P(('dp', 'tensor')), may hold values from -3 to 3
- grad_out: bfloat16 [16384, 768], P(('dp', 'tensor')), may hold values from -6 to 6
Outputs:
- activations: bfloat16 [16384, 768], P(('dp', 'tensor'))
- input_grad: float32 [16384, 768], P(('dp', 'tensor'))
- teacher_query_weight_grad: float32 [768, 768], P('dp', 'tensor')
- teacher_query_bias_grad: float32 [2, 384], P('tensor', 'dp')
- teacher_key_weight_grad: float32 [768, 768], P('dp', 'tensor')
- teacher_value_weight_grad: float32 [768, 768], P('dp', 'tensor')
- teacher_value_bias_grad: float32 [2, 384], P('tensor', 'dp')
- teacher_output_weight_grad: float32 [768, 768], P('tensor', 'dp')
- teacher_output_bias_grad: float32 [768], P(('dp', 'tensor'))
- teacher_first_gain_grad: float32 [768], P(('dp', 'tensor'))
- teacher_first_shift_grad: float32 [768], P(('dp', 'tensor'))
- teacher_up_weight_grad: float32 [768, 3072], P('dp', 'tensor')
- teacher_up_bias_grad: float32 [2, 1536], P('tensor', 'dp')
- teacher_down_weight_grad: float32 [3072, 768], P('tensor', 'dp')
- teacher_down_bias_grad: float32 [768], P(('dp', 'tensor'))
- teacher_second_gain_grad: float32 [768], P(('dp', 'tensor'))
- teacher_second_shift_grad: float32 [768], P(('dp', 'tensor'))
- student_query_weight_grad: float32 [768, 768], P('dp', 'tensor')
- student_query_bias_grad: float32 [2, 384], P('tensor', 'dp')
- student_key_weight_grad: float32 [768, 768], P('dp', 'tensor')
- student_value_weight_grad: float32 [768, 768], P('dp', 'tensor')
- student_value_bias_grad: float32 [2, 384], P('tensor', 'dp')
- student_output_weight_grad: float32 [768, 768], P('tensor', 'dp')
- student_output_bias_grad: float32 [768], P(('dp', 'tensor'))
- student_first_gain_grad: float32 [768], P(('dp', 'tensor'))
- student_first_shift_grad: float32 [768], P(('dp', 'tensor'))
- student_up_weight_grad: float32 [768, 3072], P('dp', 'tensor')
- student_up_bias_grad: float32 [2, 1536], P('tensor', 'dp')
- student_down_weight_grad: float32 [3072, 768], P('tensor', 'dp')
- student_down_bias_grad: float32 [768], P(('dp', 'tensor'))
- student_second_gain_grad: float32 [768], P(('dp', 'tensor'))
- student_second_shift_grad: float32 [768], P(('dp', 'tensor'))
Inputs may be any that keep to these rules, and one draw needn't show every extreme that they name: Sequence s holds valid tokens in its first lengths[s] of 512 slots, the rest is padding; some sequence is full and some has 128.
All inputs are finite; a program needn't handle non-finite values.
Results may differ from a plain program's by a relative error of at most 0.039.
Values may be sent and summed in bfloat16 or wider, within the bound.
A program may use at most 192 MiB of HBM per device.

v0:
```python
import jax
import jax.numpy as jnp
from jax import lax
from jax.sharding import PartitionSpec as P

HEAD = 64


EPS = 1e-06
NEG = -1e30


def layer_norm(residual, norm_gain, norm_shift):
    average = jnp.mean(residual, axis=-1, keepdims=True)
    centred = residual - average
    variance = jnp.mean(centred * centred, axis=-1, keepdims=True)
    return centred * lax.rsqrt(variance + EPS) * norm_gain + norm_shift


def gelu_exact(pre_act):
    return jax.nn.gelu(pre_act, approximate=False)


def product(first_op, second_op):
    return jnp.dot(first_op, second_op, preferred_element_type=jnp.float32)


def product_tn(first_op, second_op):
    return lax.dot_general(
        first_op, second_op, (((0,), (0,)), ((), ())), preferred_element_type=jnp.float32
    )


def product_nt(first_op, second_op):
    return lax.dot_general(
        first_op, second_op, (((1,), (1,)), ((), ())), preferred_element_type=jnp.float32
    )


def gather_rows(shard):
    return lax.all_gather(shard, "tensor", axis=0, tiled=True)


def sum_rows(part_sums):
    return lax.psum_scatter(
        part_sums.astype(jnp.bfloat16), "tensor", scatter_dimension=0, tiled=True
    ).astype(jnp.float32)


def gather_grads(shard):
    return lax.all_gather(shard, "tensor", axis=0, tiled=True)


def sum_grads(part_sums):
    return lax.psum_scatter(
        part_sums.astype(jnp.bfloat16), "tensor", scatter_dimension=0, tiled=True
    ).astype(jnp.float32)


def block_view(matrix, start, count, head_dim):
    piece = lax.dynamic_slice_in_dim(matrix, start, count, 0)
    return piece.reshape(count, matrix.shape[1] // head_dim, head_dim)


def score_block(queries, key_rows, valid_keys, scale):
    raw_scores = (
        jnp.einsum("qhd,khd->hqk", queries, key_rows, preferred_element_type=jnp.float32) * scale
    )
    return jnp.where(valid_keys[None, None, :], raw_scores, NEG)


def attend_forward(queries, key_rows, value_rows, valid_keys, head_dim):
    group_rows, width = queries.shape
    seq_len = valid_keys.shape[1]
    block = min(512, seq_len)
    per_seq = seq_len // block
    scale = head_dim ** (-0.5)

    def one_block(index):
        which = index // per_seq
        query_blk = block_view(queries, index * block, block, head_dim)
        key_seq = block_view(key_rows, which * seq_len, seq_len, head_dim)
        value_seq = block_view(value_rows, which * seq_len, seq_len, head_dim)
        valid_row = lax.dynamic_index_in_dim(valid_keys, which, 0, keepdims=False)
        scores = score_block(query_blk, key_seq, valid_row, scale)
        row_max = jnp.max(scores, axis=-1, keepdims=True)
        exponent = jnp.exp(scores - row_max)
        row_total = jnp.sum(exponent, axis=-1, keepdims=True)
        attn_probs = (exponent / row_total).astype(jnp.bfloat16)
        outcome = jnp.einsum(
            "hqk,khd->qhd", attn_probs, value_seq, preferred_element_type=jnp.float32
        )
        return (
            outcome.reshape(block, width).astype(jnp.bfloat16),
            (row_max + jnp.log(row_total))[..., 0],
        )

    attended, log_sums = lax.map(one_block, jnp.arange(group_rows // block))
    return (attended.reshape(group_rows, width), log_sums)


def attend_backward(queries, key_rows, value_rows, d_attended, log_sums, valid_keys, head_dim):
    group_rows, width = queries.shape
    seq_len = valid_keys.shape[1]
    block = min(512, seq_len)
    per_seq = seq_len // block
    scale = head_dim ** (-0.5)

    def one_block(carried, index):
        grad_keys, grad_values = carried
        which = index // per_seq
        query_blk = block_view(queries, index * block, block, head_dim)
        key_seq = block_view(key_rows, which * seq_len, seq_len, head_dim)
        value_seq = block_view(value_rows, which * seq_len, seq_len, head_dim)
        grad_blk = block_view(d_attended, index * block, block, head_dim)
        valid_row = lax.dynamic_index_in_dim(valid_keys, which, 0, keepdims=False)
        scores = score_block(query_blk, key_seq, valid_row, scale)
        attn_probs = jnp.exp(scores - log_sums[index][..., None])
        d_probs = jnp.einsum(
            "qhd,khd->hqk", grad_blk, value_seq, preferred_element_type=jnp.float32
        )
        d_scores = (
            attn_probs * (d_probs - jnp.sum(attn_probs * d_probs, axis=-1, keepdims=True))
        ).astype(jnp.bfloat16)
        d_query = (
            jnp.einsum("hqk,khd->qhd", d_scores, key_seq, preferred_element_type=jnp.float32)
            * scale
        )
        d_key = (
            jnp.einsum("hqk,qhd->khd", d_scores, query_blk, preferred_element_type=jnp.float32)
            * scale
        )
        d_value = jnp.einsum(
            "hqk,qhd->khd",
            attn_probs.astype(jnp.bfloat16),
            grad_blk,
            preferred_element_type=jnp.float32,
        )
        key_start = which * seq_len
        grad_keys = lax.dynamic_update_slice_in_dim(
            grad_keys,
            lax.dynamic_slice_in_dim(grad_keys, key_start, seq_len, 0)
            + d_key.reshape(seq_len, width),
            key_start,
            0,
        )
        grad_values = lax.dynamic_update_slice_in_dim(
            grad_values,
            lax.dynamic_slice_in_dim(grad_values, key_start, seq_len, 0)
            + d_value.reshape(seq_len, width),
            key_start,
            0,
        )
        return ((grad_keys, grad_values), d_query.reshape(block, width).astype(jnp.bfloat16))

    zero_grads = jnp.zeros((group_rows, width), jnp.float32)
    (grad_keys, grad_values), d_queries = lax.scan(
        one_block, (zero_grads, zero_grads), jnp.arange(group_rows // block)
    )
    return (
        d_queries.reshape(group_rows, width),
        grad_keys.astype(jnp.bfloat16),
        grad_values.astype(jnp.bfloat16),
    )


def layer_forward(layer_rows, weights, norms, valid_keys, head_dim):
    query_w, query_b, key_w, value_w, value_b, out_w, up_w, up_b, down_w = weights
    out_b, gain_one, shift_one, down_b, gain_two, shift_two = norms
    layer_group = gather_rows(layer_rows)
    queries = (product(layer_group, query_w) + query_b.astype(jnp.float32)).astype(jnp.bfloat16)
    key_rows = product(layer_group, key_w).astype(jnp.bfloat16)
    value_rows = (product(layer_group, value_w) + value_b.astype(jnp.float32)).astype(jnp.bfloat16)
    attended, log_sums = attend_forward(queries, key_rows, value_rows, valid_keys, head_dim)
    branch = sum_rows(product(attended, out_w))
    resid_one = layer_rows.astype(jnp.float32) + branch + out_b
    hidden = layer_norm(resid_one, gain_one, shift_one).astype(jnp.bfloat16)
    hidden_group = gather_rows(hidden)
    upward = product(hidden_group, up_w) + up_b.astype(jnp.float32)
    active = gelu_exact(upward).astype(jnp.bfloat16)
    resid_two = hidden.astype(jnp.float32) + sum_rows(product(active, down_w)) + down_b
    result = layer_norm(resid_two, gain_two, shift_two)
    saved = (
        layer_group,
        queries,
        key_rows,
        value_rows,
        attended,
        log_sums,
        resid_one,
        hidden_group,
        upward,
        active,
        resid_two,
    )
    return (result, saved)


def layer_backward(d_result, weights, norms, saved, valid_keys, head_dim):
    query_w, query_b, key_w, value_w, value_b, out_w, up_w, up_b, down_w = weights
    out_b, gain_one, shift_one, down_b, gain_two, shift_two = norms
    (
        layer_group,
        queries,
        key_rows,
        value_rows,
        attended,
        log_sums,
        resid_one,
        hidden_group,
        upward,
        active,
        resid_two,
    ) = saved
    norm_value, norm_two_back = jax.vjp(layer_norm, resid_two, gain_two, shift_two)
    d_resid_two, d_gain_two, d_shift_two = norm_two_back(d_result)
    d_down_group = gather_grads(d_resid_two.astype(jnp.bfloat16))
    d_down_w = product_tn(active, d_down_group)
    gelu_value, gelu_back = jax.vjp(gelu_exact, upward)
    d_upward = gelu_back(product_nt(d_down_group, down_w))[0].astype(jnp.bfloat16)
    d_up_w = product_tn(hidden_group, d_upward)
    d_up_b = jnp.sum(d_upward, axis=0, keepdims=True, dtype=jnp.float32)
    d_hidden = d_resid_two + sum_grads(product_nt(d_upward, up_w))
    first_value, norm_one_back = jax.vjp(layer_norm, resid_one, gain_one, shift_one)
    d_resid_one, d_gain_one, d_shift_one = norm_one_back(d_hidden)
    d_branch_group = gather_grads(d_resid_one.astype(jnp.bfloat16))
    d_out_w = product_tn(attended, d_branch_group)
    d_attended = product_nt(d_branch_group, out_w).astype(jnp.bfloat16)
    d_queries, d_keys, d_values = attend_backward(
        queries, key_rows, value_rows, d_attended, log_sums, valid_keys, head_dim
    )
    d_query_w = product_tn(layer_group, d_queries)
    d_query_b = jnp.sum(d_queries, axis=0, keepdims=True, dtype=jnp.float32)
    d_key_w = product_tn(layer_group, d_keys)
    d_value_w = product_tn(layer_group, d_values)
    d_value_b = jnp.sum(d_values, axis=0, keepdims=True, dtype=jnp.float32)
    d_group = (
        product_nt(d_queries, query_w) + product_nt(d_keys, key_w) + product_nt(d_values, value_w)
    )
    d_input = d_resid_one + sum_grads(d_group)
    weight_terms = (
        d_query_w,
        d_query_b,
        d_key_w,
        d_value_w,
        d_value_b,
        d_out_w,
        d_up_w,
        d_up_b,
        d_down_w,
    )
    norm_terms = (
        jnp.sum(d_resid_one, axis=0),
        d_gain_one,
        d_shift_one,
        jnp.sum(d_resid_two, axis=0),
        d_gain_two,
        d_shift_two,
    )
    return (d_input, weight_terms, norm_terms)


def local(
    inputs,
    lengths,
    teacher_query_weight,
    teacher_query_bias,
    teacher_key_weight,
    teacher_value_weight,
    teacher_value_bias,
    teacher_output_weight,
    teacher_output_bias,
    teacher_first_gain,
    teacher_first_shift,
    teacher_up_weight,
    teacher_up_bias,
    teacher_down_weight,
    teacher_down_bias,
    teacher_second_gain,
    teacher_second_shift,
    student_query_weight,
    student_query_bias,
    student_key_weight,
    student_value_weight,
    student_value_bias,
    student_output_weight,
    student_output_bias,
    student_first_gain,
    student_first_shift,
    student_up_weight,
    student_up_bias,
    student_down_weight,
    student_down_bias,
    student_second_gain,
    student_second_shift,
    grad_out,
):
    head_dim = HEAD
    stored = (
        (
            (
                teacher_query_weight,
                teacher_query_bias,
                teacher_key_weight,
                teacher_value_weight,
                teacher_value_bias,
                teacher_output_weight,
                teacher_up_weight,
                teacher_up_bias,
                teacher_down_weight,
            ),
            (
                teacher_output_bias,
                teacher_first_gain,
                teacher_first_shift,
                teacher_down_bias,
                teacher_second_gain,
                teacher_second_shift,
            ),
        ),
        (
            (
                student_query_weight,
                student_query_bias,
                student_key_weight,
                student_value_weight,
                student_value_bias,
                student_output_weight,
                student_up_weight,
                student_up_bias,
                student_down_weight,
            ),
            (
                student_output_bias,
                student_first_gain,
                student_first_shift,
                student_down_bias,
                student_second_gain,
                student_second_shift,
            ),
        ),
    )
    row_count = inputs.shape[0]
    seq_count = lengths.shape[0]
    group_rows = row_count * lax.axis_size("tensor")
    seq_len = group_rows // seq_count
    slots = lax.axis_index("tensor") * row_count + jnp.arange(row_count)
    which_seq = slots // seq_len
    place = slots % seq_len
    table = which_seq[:, None] == jnp.arange(seq_count)[None, :]
    limits = jnp.sum(jnp.where(table, lengths[None, :], 0), axis=1)
    row_mask = (place < limits).astype(jnp.float32)[:, None]
    valid_keys = jnp.arange(seq_len)[None, :] < lengths[:, None]
    kept = []
    current = inputs
    result = None
    for layer_index in range(2):
        mats = stored[layer_index][0]
        norm_shards = stored[layer_index][1]
        weights = (
            lax.all_gather(mats[0], "dp", axis=0, tiled=True),
            lax.all_gather(mats[1], "dp", axis=1, tiled=True),
            lax.all_gather(mats[2], "dp", axis=0, tiled=True),
            lax.all_gather(mats[3], "dp", axis=0, tiled=True),
            lax.all_gather(mats[4], "dp", axis=1, tiled=True),
            lax.all_gather(mats[5], "dp", axis=1, tiled=True),
            lax.all_gather(mats[6], "dp", axis=0, tiled=True),
            lax.all_gather(mats[7], "dp", axis=1, tiled=True),
            lax.all_gather(mats[8], "dp", axis=1, tiled=True),
        )
        norms = (
            lax.all_gather(norm_shards[0], ("dp", "tensor"), axis=0, tiled=True),
            lax.all_gather(norm_shards[1], ("dp", "tensor"), axis=0, tiled=True),
            lax.all_gather(norm_shards[2], ("dp", "tensor"), axis=0, tiled=True),
            lax.all_gather(norm_shards[3], ("dp", "tensor"), axis=0, tiled=True),
            lax.all_gather(norm_shards[4], ("dp", "tensor"), axis=0, tiled=True),
            lax.all_gather(norm_shards[5], ("dp", "tensor"), axis=0, tiled=True),
        )
        result, saved = layer_forward(current, weights, norms, valid_keys, head_dim)
        kept.append((weights, norms, saved))
        current = result.astype(jnp.bfloat16)
    activations = (result * row_mask).astype(jnp.bfloat16)
    d_current = grad_out.astype(jnp.float32) * row_mask
    weight_parts = [None, None]
    norm_parts = [None, None]
    for layer_index in (1, 0):
        weights, norms, saved = kept[layer_index]
        mats = stored[layer_index][0]
        weights = (
            lax.all_gather(mats[0], "dp", axis=0, tiled=True),
            lax.all_gather(mats[1], "dp", axis=1, tiled=True),
            lax.all_gather(mats[2], "dp", axis=0, tiled=True),
            lax.all_gather(mats[3], "dp", axis=0, tiled=True),
            lax.all_gather(mats[4], "dp", axis=1, tiled=True),
            lax.all_gather(mats[5], "dp", axis=1, tiled=True),
            lax.all_gather(mats[6], "dp", axis=0, tiled=True),
            lax.all_gather(mats[7], "dp", axis=1, tiled=True),
            lax.all_gather(mats[8], "dp", axis=1, tiled=True),
        )
        d_current, weight_terms, norm_terms = layer_backward(
            d_current, weights, norms, saved, valid_keys, head_dim
        )
        norm_parts[layer_index] = (
            lax.psum_scatter(norm_terms[0], ("dp", "tensor"), scatter_dimension=0, tiled=True),
            lax.psum_scatter(norm_terms[1], ("dp", "tensor"), scatter_dimension=0, tiled=True),
            lax.psum_scatter(norm_terms[2], ("dp", "tensor"), scatter_dimension=0, tiled=True),
            lax.psum_scatter(norm_terms[3], ("dp", "tensor"), scatter_dimension=0, tiled=True),
            lax.psum_scatter(norm_terms[4], ("dp", "tensor"), scatter_dimension=0, tiled=True),
            lax.psum_scatter(norm_terms[5], ("dp", "tensor"), scatter_dimension=0, tiled=True),
        )
        weight_parts[layer_index] = (
            lax.psum_scatter(weight_terms[0], "dp", scatter_dimension=0, tiled=True),
            lax.psum_scatter(weight_terms[1], "dp", scatter_dimension=1, tiled=True),
            lax.psum_scatter(weight_terms[2], "dp", scatter_dimension=0, tiled=True),
            lax.psum_scatter(weight_terms[3], "dp", scatter_dimension=0, tiled=True),
            lax.psum_scatter(weight_terms[4], "dp", scatter_dimension=1, tiled=True),
            lax.psum_scatter(weight_terms[5], "dp", scatter_dimension=1, tiled=True),
            lax.psum_scatter(weight_terms[6], "dp", scatter_dimension=0, tiled=True),
            lax.psum_scatter(weight_terms[7], "dp", scatter_dimension=1, tiled=True),
            lax.psum_scatter(weight_terms[8], "dp", scatter_dimension=1, tiled=True),
        )
    ordered = []
    for layer_index in range(2):
        wsum = weight_parts[layer_index]
        nsum = norm_parts[layer_index]
        ordered.extend(
            [
                wsum[0],
                wsum[1],
                wsum[2],
                wsum[3],
                wsum[4],
                wsum[5],
                nsum[0],
                nsum[1],
                nsum[2],
                wsum[6],
                wsum[7],
                wsum[8],
                nsum[3],
                nsum[4],
                nsum[5],
            ]
        )
    return (
        activations,
        d_current,
        ordered[0],
        ordered[1],
        ordered[2],
        ordered[3],
        ordered[4],
        ordered[5],
        ordered[6],
        ordered[7],
        ordered[8],
        ordered[9],
        ordered[10],
        ordered[11],
        ordered[12],
        ordered[13],
        ordered[14],
        ordered[15],
        ordered[16],
        ordered[17],
        ordered[18],
        ordered[19],
        ordered[20],
        ordered[21],
        ordered[22],
        ordered[23],
        ordered[24],
        ordered[25],
        ordered[26],
        ordered[27],
        ordered[28],
        ordered[29],
    )


def solution(mesh):
    return jax.shard_map(
        local,
        mesh=mesh,
        in_specs=(
            P(("dp", "tensor"), None),
            P("dp"),
            P("dp", "tensor"),
            P("tensor", "dp"),
            P("dp", "tensor"),
            P("dp", "tensor"),
            P("tensor", "dp"),
            P("tensor", "dp"),
            P(("dp", "tensor")),
            P(("dp", "tensor")),
            P(("dp", "tensor")),
            P("dp", "tensor"),
            P("tensor", "dp"),
            P("tensor", "dp"),
            P(("dp", "tensor")),
            P(("dp", "tensor")),
            P(("dp", "tensor")),
            P("dp", "tensor"),
            P("tensor", "dp"),
            P("dp", "tensor"),
            P("dp", "tensor"),
            P("tensor", "dp"),
            P("tensor", "dp"),
            P(("dp", "tensor")),
            P(("dp", "tensor")),
            P(("dp", "tensor")),
            P("dp", "tensor"),
            P("tensor", "dp"),
            P("tensor", "dp"),
            P(("dp", "tensor")),
            P(("dp", "tensor")),
            P(("dp", "tensor")),
            P(("dp", "tensor"), None),
        ),
        out_specs=(
            P(("dp", "tensor"), None),
            P(("dp", "tensor"), None),
            P("dp", "tensor"),
            P("tensor", "dp"),
            P("dp", "tensor"),
            P("dp", "tensor"),
            P("tensor", "dp"),
            P("tensor", "dp"),
            P(("dp", "tensor")),
            P(("dp", "tensor")),
            P(("dp", "tensor")),
            P("dp", "tensor"),
            P("tensor", "dp"),
            P("tensor", "dp"),
            P(("dp", "tensor")),
            P(("dp", "tensor")),
            P(("dp", "tensor")),
            P("dp", "tensor"),
            P("tensor", "dp"),
            P("dp", "tensor"),
            P("dp", "tensor"),
            P("tensor", "dp"),
            P("tensor", "dp"),
            P(("dp", "tensor")),
            P(("dp", "tensor")),
            P(("dp", "tensor")),
            P("dp", "tensor"),
            P("tensor", "dp"),
            P("tensor", "dp"),
            P(("dp", "tensor")),
            P(("dp", "tensor")),
            P(("dp", "tensor")),
        ),
        check_vma=False,
    )
```

profile of v0, /device:TPU:0, one launch (start us, length us, event | category | flops | bytes accessed | tf_op | source)
XLA Modules:
  0.0 1884.7 jit_solution(3632678534955139546)
XLA Ops:
  16.6 63.0 %all-reduce.37 = (bf16[384]{0:T(512)(128)(2,1)S(1)}, bf16[384]{0:T(512)(128)(2,1)S(1)}, bf16[1536]{0:T(1024)(128)(2,1)S(1)}, bf16[384]{0:T(512)(128)(2,1)S(1)}, ...) all-reduce(bf16[384]{0:T(512)(128)(2,1)S(1)} %dynamic-update-slice, ...), channel_id=1, replica_groups=mesh['dp'=16,'tensor'=2] {'dp'}, use_global_device_ids=true, to_apply=%add | all-reduce | flops 4608 | bytes 18432
  80.3 19.2 %all_gather.127 = bf16[768,384]{1,0:T(8,128)(2,1)S(1)} all-gather(bf16[48,384]{1,0:T(8,128)(2,1)} %param.46), channel_id=1, replica_groups=mesh['dp'=16,'tensor'=2] {'dp'}, dimensions={0}, use_global_device_ids=true | all-gather | bytes 626688 | tf_op jit(solution)/shard_map/all_gather | solution.py:364
  99.5 22.1 %all_gather.129 = bf16[768,384]{1,0:T(8,128)(2,1)} all-gather(bf16[48,384]{1,0:T(8,128)(2,1)} %param.43), channel_id=1, replica_groups=mesh['dp'=16,'tensor'=2] {'dp'}, dimensions={0}, use_global_device_ids=true | all-gather | bytes 626688 | tf_op jit(solution)/shard_map/all_gather | solution.py:361
  121.6 20.4 %all_gather.131 = bf16[768,384]{1,0:T(8,128)(2,1)} all-gather(bf16[48,384]{1,0:T(8,128)(2,1)S(1)} %copy-done.81), channel_id=1, replica_groups=mesh['dp'=16,'tensor'=2] {'dp'}, dimensions={0}, use_global_device_ids=true | all-gather | bytes 626688 | tf_op jit(solution)/shard_map/all_gather | solution.py:363
  142.0 21.9 %all_gather.132 = bf16[384,768]{0,1:T(8,128)(2,1)} all-gather(bf16[384,48]{0,1:T(8,128)(2,1)S(1)} %copy-done.82), channel_id=1, replica_groups=mesh['dp'=16,'tensor'=2] {'dp'}, dimensions={1}, use_global_device_ids=true | all-gather | bytes 626688 | tf_op jit(solution)/shard_map/all_gather | solution.py:366
  179.0 20.1 %while.60 = (s32[]{:T(128)}, bf16[2,512,384]{2,1,0:T(8,128)(2,1)S(1)}, f32[2,6,512]{2,1,0:T(8,128)}, s32[2]{0:T(128)S(1)}, bf16[1024,384]{0,1:T(8,128)(2,1)S(1)}...) while((s32[]{:T(128)}, ...), condition=%wide.region_3.4_spmd, body=%wide.region_0.3_spmd.sunk | while | flops 421721088 | bytes 24485096 | solution.py:98
  204.8 38.7 %all-reduce.35 = (f32[768]{0:T(1024)}, f32[768]{0:T(1024)S(1)}, f32[768]{0:T(1024)S(1)}, f32[768]{0:T(1024)S(1)}, f32[768]{0:T(1024)S(1)}, /*index=5*/f32[768]{0...) all-reduce(f32[768]{0:T(1024)S(1)} %dynamic-update-slice.16, ...), channel_id=1, replica_groups=mesh['dp'=16,'tensor'=2] {'dp','tensor'}, use_global_device_ids=true, to_apply=%add.16 | all-reduce | flops 8448 | bytes 67584
  247.7 27.9 %all-gather.15.cloned.1.call-done = bf16[1024,768]{1,0:T(8,128)(2,1)} async-done(((bf16[512,768]{1,0:T(8,128)(2,1)}), bf16[1024,768]{1,0:T(8,128)(2,1)}) %all-gather.15.cloned.1.call-update) | async-done | bytes 1572880 | tf_op jit(solution)/shard_map/all_gather | solution.py:41
  275.6 20.0 %multiply_convert_fusion.3 = (bf16[1024,1536]{1,0:T(8,128)(2,1)}, f32[1024,1536]{1,0:T(8,128)}, f32[1024,1536]{1,0:T(8,128)}) fusion(f32[1536]{0:T(1024)S(1)} %add.616, bf16[1024,768]{1,0:T(8,128)(2,1)} %all-gather.15.cloned.1.call-done, bf16[768,1536]{1,0:T(8,128)(2,1)} %all-gather.17.cloned.1.call-done), kind=kOutput, calls=%fused_computation.95 | convolution fusion | flops 2519728128 | bytes 19666944 | tf_op jit(solution)/shard_map/dot_general | solution.py:25
  295.6 25.2 %all-gather.19.cloned.1.call-done = bf16[1536,768]{0,1:T(8,128)(2,1)} async-done(((bf16[1536,48]{0,1:T(8,128)(2,1)}), bf16[1536,768]{0,1:T(8,128)(2,1)}) %all-gather.19.cloned.1.call-update) | async-done | bytes 2359312 | tf_op jit(solution)/shard_map/all_gather | solution.py:369
  327.7 24.3 %reduce-scatter.39.cloned.1.call-done = bf16[512,768]{1,0:T(8,128)(2,1)} async-done(((bf16[1024,768]{1,0:T(8,128)(2,1)}), bf16[512,768]{1,0:T(8,128)(2,1)}) %reduce-scatter.39.cloned.1.call-update) | async-done | bytes 786448 | tf_op jit(solution)/shard_map/reduce_scatter | solution.py:45
  355.5 23.1 %all_gather.144 = bf16[768,384]{1,0:T(8,128)(2,1)S(1)} all-gather(bf16[48,384]{1,0:T(8,128)(2,1)S(1)} %copy-done.83), channel_id=1, replica_groups=mesh['dp'=16,'tensor'=2] {'dp'}, dimensions={0}, use_global_device_ids=true | all-gather | bytes 626688 | tf_op jit(solution)/shard_map/all_gather | solution.py:364
  378.7 19.0 %all_gather.146 = bf16[768,384]{1,0:T(8,128)(2,1)S(1)} all-gather(bf16[48,384]{1,0:T(8,128)(2,1)S(1)} %copy-done.84), channel_id=1, replica_groups=mesh['dp'=16,'tensor'=2] {'dp'}, dimensions={0}, use_global_device_ids=true | all-gather | bytes 626688 | tf_op jit(solution)/shard_map/all_gather | solution.py:361
  397.7 21.8 %all_gather.148 = bf16[768,384]{1,0:T(8,128)(2,1)} all-gather(bf16[48,384]{1,0:T(8,128)(2,1)S(1)} %copy-done.85), channel_id=1, replica_groups=mesh['dp'=16,'tensor'=2] {'dp'}, dimensions={0}, use_global_device_ids=true | all-gather | bytes 626688 | tf_op jit(solution)/shard_map/all_gather | solution.py:363
  419.5 20.4 %all_gather.149 = bf16[384,768]{0,1:T(8,128)(2,1)} all-gather(bf16[384,48]{0,1:T(8,128)(2,1)S(1)} %copy-done.86), channel_id=1, replica_groups=mesh['dp'=16,'tensor'=2] {'dp'}, dimensions={1}, use_global_device_ids=true | all-gather | bytes 626688 | tf_op jit(solution)/shard_map/all_gather | solution.py:366
  452.0 20.1 %while.61 = (s32[]{:T(128)}, bf16[2,512,384]{2,1,0:T(8,128)(2,1)}, f32[2,6,512]{2,1,0:T(8,128)S(1)}, s32[2]{0:T(128)S(1)}, bf16[1024,384]{0,1:T(8,128)(2,1)S(1)}...) while((s32[]{:T(128)}, bf16[2,512,384]{2,1,0:T(8,128)(2,1)}, ...), condition=%wide.region_13.14_spmd, body=%wide.region_10.13_spmd.sunk | while | flops 421721088 | bytes 24493288 | solution.py:98
  477.4 22.9 %reduce-scatter.41.cloned.1.call-done = bf16[512,768]{1,0:T(8,128)(2,1)} async-done(((bf16[1024,768]{1,0:T(8,128)(2,1)}), bf16[512,768]{1,0:T(8,128)(2,1)}) %reduce-scatter.41.cloned.1.call-update) | async-done | bytes 786448 | tf_op jit(solution)/shard_map/reduce_scatter | solution.py:45
  504.5 15.6 all-gather.25.cloned.1.call-done
  520.2 27.2 %all-gather.23.cloned.1.call-done = bf16[1024,768]{1,0:T(8,128)(2,1)} async-done(((bf16[512,768]{1,0:T(8,128)(2,1)}), bf16[1024,768]{1,0:T(8,128)(2,1)}) %all-gather.23.cloned.1.call-update) | async-done | bytes 1572880 | tf_op jit(solution)/shard_map/all_gather | solution.py:41
  547.4 20.0 %multiply_convert_fusion.2 = (bf16[1024,1536]{1,0:T(8,128)(2,1)}, f32[1024,1536]{1,0:T(8,128)}, f32[1024,1536]{1,0:T(8,128)}) fusion(f32[1536]{0:T(1024)S(1)} %add.619, bf16[1024,768]{1,0:T(8,128)(2,1)} %all-gather.23.cloned.1.call-done, bf16[768,1536]{1,0:T(8,128)(2,1)} %all-gather.25.cloned.1.call-done), kind=kOutput, calls=%fused_computation.82 | convolution fusion | flops 2519728128 | bytes 19666944 | tf_op jit(solution)/shard_map/dot_general | solution.py:25
  567.4 25.3 %all-gather.27.cloned.1.call-done = bf16[1536,768]{0,1:T(8,128)(2,1)} async-done(((bf16[1536,48]{0,1:T(8,128)(2,1)}), bf16[1536,768]{0,1:T(8,128)(2,1)}) %all-gather.27.cloned.1.call-update) | async-done | bytes 2359312 | tf_op jit(solution)/shard_map/all_gather | solution.py:369
  599.9 24.0 %reduce-scatter.43.cloned.1.call-done = bf16[512,768]{1,0:T(8,128)(2,1)} async-done(((bf16[1024,768]{1,0:T(8,128)(2,1)}), bf16[512,768]{1,0:T(8,128)(2,1)}) %reduce-scatter.43.cloned.1.call-update) | async-done | bytes 786448 | tf_op jit(solution)/shard_map/reduce_scatter | solution.py:45
  630.9 27.1 %all-gather.29.cloned.1.call-done = bf16[1024,768]{1,0:T(8,128)(2,1)} async-done(((bf16[512,768]{1,0:T(8,128)(2,1)}), bf16[1024,768]{1,0:T(8,128)(2,1)}) %all-gather.29.cloned.1.call-update) | async-done | bytes 1572880 | tf_op jit(solution)/shard_map/all_gather | solution.py:51
  658.0 10.3 convert_reduce_fusion
  673.8 26.2 %reduce-scatter.45.cloned.1.call-done = bf16[512,768]{1,0:T(8,128)(2,1)} async-done(((bf16[1024,768]{1,0:T(8,128)(2,1)}), bf16[512,768]{1,0:T(8,128)(2,1)}) %reduce-scatter.45.cloned.1.call-update) | async-done | bytes 786448 | tf_op jit(solution)/shard_map/reduce_scatter | solution.py:55
  708.3 27.1 %all-gather.31.cloned.1.call-done = bf16[1024,768]{1,0:T(8,128)(2,1)} async-done(((bf16[512,768]{1,0:T(8,128)(2,1)}), bf16[1024,768]{1,0:T(8,128)(2,1)}) %all-gather.31.cloned.1.call-update) | async-done | bytes 1572880 | tf_op jit(solution)/shard_map/all_gather | solution.py:51
  741.2 42.6 %while.62 = (s32[]{:T(128)}, f32[1024,384]{0,1:T(8,128)}, f32[1024,384]{0,1:T(8,128)S(1)}, bf16[2,512,384]{1,2,0:T(8,128)(2,1)}, s32[2]{0:T(128)S(1)}, /*index=5...) while((s32[]{:T(128)}, f32[1024,384]{0,1:T(8,128)}, ...), condition=%wide.region_28.29_spmd, body=%wide.region_26.28_spmd.sunk | while | flops 1031205888 | bytes 102325712 | solution.py:157
  791.6 25.6 %reduce-scatter.47.cloned.1.call-done = bf16[512,768]{1,0:T(8,128)(2,1)} async-done(((bf16[1024,768]{1,0:T(8,128)(2,1)}), bf16[512,768]{1,0:T(8,128)(2,1)}) %reduce-scatter.47.cloned.1.call-update) | async-done | bytes 786448 | tf_op jit(solution)/shard_map/reduce_scatter | solution.py:55
  823.3 27.3 %all-gather.33.cloned.1.call-done = bf16[1024,768]{1,0:T(8,128)(2,1)} async-done(((bf16[512,768]{1,0:T(8,128)(2,1)}), bf16[1024,768]{1,0:T(8,128)(2,1)}) %all-gather.33.cloned.1.call-update) | async-done | bytes 1572880 | tf_op jit(solution)/shard_map/all_gather | solution.py:51
  850.6 7.8 convert_reduce_fusion.1
  864.0 26.2 %reduce-scatter.49.cloned.1.call-done = bf16[512,768]{1,0:T(8,128)(2,1)} async-done(((bf16[1024,768]{1,0:T(8,128)(2,1)}), bf16[512,768]{1,0:T(8,128)(2,1)}) %reduce-scatter.49.cloned.1.call-update) | async-done | bytes 786448 | tf_op jit(solution)/shard_map/reduce_scatter | solution.py:55
  899.0 24.4 %all-gather.35.cloned.1.call-done = bf16[1024,768]{1,0:T(8,128)(2,1)} async-done(((bf16[512,768]{1,0:T(8,128)(2,1)}), bf16[1024,768]{1,0:T(8,128)(2,1)}) %all-gather.35.cloned.1.call-update) | async-done | bytes 1572880 | tf_op jit(solution)/shard_map/all_gather | solution.py:51
  929.7 49.6 %while.63 = (s32[]{:T(128)}, f32[1024,384]{0,1:T(8,128)}, f32[1024,384]{0,1:T(8,128)S(1)}, bf16[2,512,384]{1,2,0:T(8,128)(2,1)}, s32[2]{0:T(128)}, /*index=5*/bf...) while((s32[]{:T(128)}, f32[1024,384]{0,1:T(8,128)}, ...), condition=%wide.region_37.38_spmd, body=%wide.region_35.37_spmd.sunk | while | flops 1031205888 | bytes 96034208 | solution.py:157
  1002.2 7.3 fusion.90
  1039.6 7.3 fusion.86
  1060.9 33.6 %all-reduce.36 = (f32[1,384]{1,0:T(1,128)S(1)}, f32[1,384]{1,0:T(1,128)S(1)}, f32[1,384]{1,0:T(1,128)S(1)}, f32[1,384]{1,0:T(1,128)S(1)}) all-reduce(f32[1,384]{1,0:T(1,128)S(1)} %broadcast_in_dim.200, f32[1,384]{1,0:T(1,128)S(1)} %broadcast_in_dim.201, ...), channel_id=11, replica_groups=mesh['dp'=16,'tensor'=2] {'dp'}, use_global_device_ids=true, to_apply=%region_41.42.clone | all-reduce | flops 1536 | bytes 12288
  1098.6 38.1 %all-reduce.34 = (f32[768]{0:T(1024)S(1)}, f32[768]{0:T(1024)S(1)}, f32[768]{0:T(1024)S(1)}, f32[768]{0:T(1024)S(1)}, f32[768]{0:T(1024)S(1)}, /*index=5*/f32[76...) all-reduce(f32[768]{0:T(1024)S(1)} %dynamic-update-slice.17, ...), channel_id=1, replica_groups=mesh['dp'=16,'tensor'=2] {'dp','tensor'}, use_global_device_ids=true, to_apply=%add.17 | all-reduce | flops 9984 | bytes 79872
  1145.2 48.6 %reduce-scatter.59.cloned.1.call-done = f32[48,384]{1,0:T(8,128)} async-done(((f32[768,384]{1,0:T(8,128)}), f32[48,384]{1,0:T(8,128)}) %reduce-scatter.59.cloned.1.call-update) | async-done | bytes 73744 | tf_op jit(solution)/shard_map/reduce_scatter | solution.py:412
  1193.8 61.3 %reduce-scatter.61.cloned.1.call-done = f32[48,384]{1,0:T(8,128)} async-done(((f32[768,384]{1,0:T(8,128)}), f32[48,384]{1,0:T(8,128)}) %reduce-scatter.61.cloned.1.call-update) | async-done | bytes 73744 | tf_op jit(solution)/shard_map/reduce_scatter | solution.py:414
  1255.0 61.2 %reduce-scatter.63.cloned.1.call-done = f32[48,384]{1,0:T(8,128)} async-done(((f32[768,384]{1,0:T(8,128)}), f32[48,384]{1,0:T(8,128)}) %reduce-scatter.63.cloned.1.call-update) | async-done | bytes 73744 | tf_op jit(solution)/shard_map/reduce_scatter | solution.py:415
  1316.2 78.9 %reduce-scatter.69.cloned.1.call-done = f32[1536,48]{0,1:T(8,128)} async-done(((f32[1536,768]{0,1:T(8,128)}), f32[1536,48]{0,1:T(8,128)}) %reduce-scatter.69.cloned.1.call-update) | async-done | bytes 294928 | tf_op jit(solution)/shard_map/reduce_scatter | solution.py:420
  1395.1 79.4 %reduce-scatter.67.cloned.1.call-done = f32[48,1536]{1,0:T(8,128)} async-done(((f32[768,1536]{1,0:T(8,128)}), f32[48,1536]{1,0:T(8,128)}) %reduce-scatter.67.cloned.1.call-update) | async-done | bytes 294928 | tf_op jit(solution)/shard_map/reduce_scatter | solution.py:418
  1474.5 61.3 %reduce-scatter.53.cloned.1.call-done = f32[384,48]{0,1:T(8,128)} async-done(((f32[384,768]{0,1:T(8,128)}), f32[384,48]{0,1:T(8,128)}) %reduce-scatter.53.cloned.1.call-update) | async-done | bytes 73744 | tf_op jit(solution)/shard_map/reduce_scatter | solution.py:417
  1535.8 61.0 %reduce-scatter.71.cloned.1.call-done = f32[48,384]{1,0:T(8,128)} async-done(((f32[768,384]{1,0:T(8,128)}), f32[48,384]{1,0:T(8,128)}) %reduce-scatter.71.cloned.1.call-update) | async-done | bytes 73744
  1596.8 61.2 %reduce-scatter.73.cloned.1.call-done = f32[48,384]{1,0:T(8,128)} async-done(((f32[768,384]{1,0:T(8,128)}), f32[48,384]{1,0:T(8,128)}) %reduce-scatter.73.cloned.1.call-update) | async-done | bytes 73744
  1658.0 61.0 %reduce-scatter.75.cloned.1.call-done = f32[48,384]{1,0:T(8,128)} async-done(((f32[768,384]{1,0:T(8,128)}), f32[48,384]{1,0:T(8,128)}) %reduce-scatter.75.cloned.1.call-update) | async-done | bytes 73744
  1719.1 78.7 %reduce-scatter.57.cloned.1.call-done = f32[1536,48]{0,1:T(8,128)} async-done(((f32[1536,768]{0,1:T(8,128)}), f32[1536,48]{0,1:T(8,128)}) %reduce-scatter.57.cloned.1.call-update) | async-done | bytes 294928 | tf_op jit(solution)/shard_map/reduce_scatter | solution.py:420
  1797.7 79.1 %reduce-scatter.55.cloned.1.call-done = f32[48,1536]{1,0:T(8,128)} async-done(((f32[768,1536]{1,0:T(8,128)}), f32[48,1536]{1,0:T(8,128)}) %reduce-scatter.55.cloned.1.call-update) | async-done | bytes 294928 | tf_op jit(solution)/shard_map/reduce_scatter | solution.py:418
  (641 shorter events, 321.5 us)
Async XLA Ops:
  8.0 113.6 %copy-start.81 = (bf16[48,384]{1,0:T(8,128)(2,1)S(1)}, bf16[48,384]{1,0:T(8,128)(2,1)}, u32[]{:S(2)}) copy-start(bf16[48,384]{1,0:T(8,128)(2,1)} %param.45) | copy-start | bytes 110596
  8.0 134.0 %copy-start.82 = (bf16[384,48]{0,1:T(8,128)(2,1)S(1)}, bf16[384,48]{0,1:T(8,128)(2,1)}, u32[]{:S(2)}) copy-start(bf16[384,48]{0,1:T(8,128)(2,1)} %param.48) | copy-start | bytes 110596
  8.1 155.9 %all-gather.13.cloned.1.call-start = ((), (), s32[]{:S(2)}) async-start(), calls=%async_computation.22 | async-start | bytes 2359296 | tf_op jit(solution)/shard_map/all_gather | solution.py:41
  8.8 234.7 %reduce-scatter.37.cloned.1.call-start = ((), (), s32[]{:S(2)}) async-start(), calls=%async_computation.23 | async-start | bytes 2359296 | tf_op jit(solution)/shard_map/reduce_scatter | solution.py:45
  99.5 67.7 %copy-start.47 = (bf16[768,384]{1,0:T(8,128)(2,1)}, bf16[768,384]{1,0:T(8,128)(2,1)S(1)}, u32[]{:S(2)}) copy-start(bf16[768,384]{1,0:T(8,128)(2,1)S(1)} %all_gather.127) | copy-start | bytes 1769476
  201.4 46.2 %all-gather.17.cloned.1.call-start = ((), (), s32[]{:S(2)}) async-start(), calls=%async_computation.25 | async-start | bytes 2506752 | tf_op jit(solution)/shard_map/all_gather | solution.py:367
  202.0 73.6 %all-gather.15.cloned.1.call-start = ((), (), s32[]{:S(2)}) async-start(), calls=%async_computation.24 | async-start | bytes 2359296 | tf_op jit(solution)/shard_map/all_gather | solution.py:41
  243.5 110.5 %copy-start.67 = (f32[768]{0:T(1024)}, f32[768]{0:T(1024)S(1)}, u32[]{:S(2)}) copy-start(f32[768]{0:T(1024)S(1)} %get-tuple-element.924) | copy-start | bytes 9220
  243.5 110.5 %copy-start.79 = (f32[768]{0:T(1024)}, f32[768]{0:T(1024)S(1)}, u32[]{:S(2)}) copy-start(f32[768]{0:T(1024)S(1)} %get-tuple-element.920) | copy-start | bytes 9220
  247.0 73.8 %all-gather.19.cloned.1.call-start = ((), (), s32[]{:S(2)}) async-start(), calls=%async_computation.26 | async-start | bytes 2506752 | tf_op jit(solution)/shard_map/all_gather | solution.py:369
  247.6 104.4 %reduce-scatter.39.cloned.1.call-start = ((), (), s32[]{:S(2)}) async-start(), calls=%async_computation.27 | async-start | bytes 2359296 | tf_op jit(solution)/shard_map/reduce_scatter | solution.py:45
  247.6 47.9 %copy-start.108 = (f32[1536]{0:T(1024)}, f32[1536]{0:T(1024)S(1)}, u32[]{:S(2)}) copy-start(f32[1536]{0:T(1024)S(1)} %add.616) | copy-start | bytes 18436
  327.2 112.7 %all-gather.21.cloned.1.call-start = ((), (), s32[]{:S(2)}) async-start(), calls=%async_computation.28 | async-start | bytes 2359296 | tf_op jit(solution)/shard_map/all_gather | solution.py:41
  355.4 64.1 %copy-start.86 = (bf16[384,48]{0,1:T(8,128)(2,1)S(1)}, bf16[384,48]{0,1:T(8,128)(2,1)}, u32[]{:S(2)}) copy-start(bf16[384,48]{0,1:T(8,128)(2,1)} %param.63) | copy-start | bytes 110596
  355.5 144.9 %reduce-scatter.41.cloned.1.call-start = ((), (), s32[]{:S(2)}) async-start(), calls=%async_computation.29 | async-start | bytes 2359296 | tf_op jit(solution)/shard_map/reduce_scatter | solution.py:45
  378.7 63.7 %copy-start.50 = (bf16[768,384]{1,0:T(8,128)(2,1)}, bf16[768,384]{1,0:T(8,128)(2,1)S(1)}, u32[]{:S(2)}) copy-start(bf16[768,384]{1,0:T(8,128)(2,1)S(1)} %all_gather.144) | copy-start | bytes 1769476
  476.5 43.7 %all-gather.25.cloned.1.call-start = ((), (), s32[]{:S(2)}) async-start(), calls=%async_computation.31 | async-start | bytes 2506752 | tf_op jit(solution)/shard_map/all_gather | solution.py:367
  477.2 70.2 %all-gather.23.cloned.1.call-start = ((), (), s32[]{:S(2)}) async-start(), calls=%async_computation.30 | async-start | bytes 2359296 | tf_op jit(solution)/shard_map/all_gather | solution.py:41
  503.7 89.0 %all-gather.27.cloned.1.call-start = ((), (), s32[]{:S(2)}) async-start(), calls=%async_computation.32 | async-start | bytes 2506752 | tf_op jit(solution)/shard_map/all_gather | solution.py:369
  504.5 119.4 %reduce-scatter.43.cloned.1.call-start = ((), (), s32[]{:S(2)}) async-start(), calls=%async_computation.33 | async-start | bytes 2359296 | tf_op jit(solution)/shard_map/reduce_scatter | solution.py:45
  599.2 58.8 %all-gather.29.cloned.1.call-start = ((), (), s32[]{:S(2)}) async-start(), calls=%async_computation.34 | async-start | bytes 2359296 | tf_op jit(solution)/shard_map/all_gather | solution.py:51
  630.6 69.4 %reduce-scatter.45.cloned.1.call-start = ((), (), s32[]{:S(2)}) async-start(), calls=%async_computation.35 | async-start | bytes 2359296 | tf_op jit(solution)/shard_map/reduce_scatter | solution.py:55
  673.8 61.6 %all-gather.31.cloned.1.call-start = ((), (), s32[]{:S(2)}) async-start(), calls=%async_computation.36 | async-start | bytes 2359296 | tf_op jit(solution)/shard_map/all_gather | solution.py:51
  708.0 109.1 %reduce-scatter.47.cloned.1.call-start = ((), (), s32[]{:S(2)}) async-start(), calls=%async_computation.37 | async-start | bytes 2359296 | tf_op jit(solution)/shard_map/reduce_scatter | solution.py:55
  791.0 59.6 %all-gather.33.cloned.1.call-start = ((), (), s32[]{:S(2)}) async-start(), calls=%async_computation.38 | async-start | bytes 2359296 | tf_op jit(solution)/shard_map/all_gather | solution.py:51
  823.3 66.9 %reduce-scatter.49.cloned.1.call-start = ((), (), s32[]{:S(2)}) async-start(), calls=%async_computation.39 | async-start | bytes 2359296 | tf_op jit(solution)/shard_map/reduce_scatter | solution.py:55
  864.0 59.5 %all-gather.35.cloned.1.call-start = ((), (), s32[]{:S(2)}) async-start(), calls=%async_computation.40 | async-start | bytes 2359296 | tf_op jit(solution)/shard_map/all_gather | solution.py:51
  896.3 158.7 %reduce-scatter.79.cloned.1.call-start = ((), (), s32[]{:S(2)}) async-start(), calls=%async_computation.55 | async-start | bytes 835584
  897.6 160.3 %reduce-scatter.77.cloned.1.call-start = ((), (), s32[]{:S(2)}) async-start(), calls=%async_computation.54 | async-start | bytes 835584
  898.8 197.0 %reduce-scatter.51.cloned.1.call-start = ((), (), s32[]{:S(2)}) async-start(), calls=%async_computation.41 | async-start | bytes 2359296 | tf_op jit(solution)/shard_map/reduce_scatter | solution.py:55
  986.1 159.1 %reduce-scatter.65.cloned.1.call-start = ((), (), s32[]{:S(2)}) async-start(), calls=%async_computation.48 | async-start | bytes 1253376 | tf_op jit(solution)/shard_map/reduce_scatter | solution.py:417
  990.7 203.1 %reduce-scatter.59.cloned.1.call-start = ((), (), s32[]{:S(2)}) async-start(), calls=%async_computation.45 | async-start | bytes 1253376 | tf_op jit(solution)/shard_map/reduce_scatter | solution.py:412
  994.2 260.8 %reduce-scatter.61.cloned.1.call-start = ((), (), s32[]{:S(2)}) async-start(), calls=%async_computation.46 | async-start | bytes 1253376 | tf_op jit(solution)/shard_map/reduce_scatter | solution.py:414
  998.6 317.6 %reduce-scatter.63.cloned.1.call-start = ((), (), s32[]{:S(2)}) async-start(), calls=%async_computation.47 | async-start | bytes 1253376 | tf_op jit(solution)/shard_map/reduce_scatter | solution.py:415
  1002.2 392.9 %reduce-scatter.69.cloned.1.call-start = ((), (), s32[]{:S(2)}) async-start(), calls=%async_computation.50 | async-start | bytes 5013504 | tf_op jit(solution)/shard_map/reduce_scatter | solution.py:420
  1009.5 465.0 %reduce-scatter.67.cloned.1.call-start = ((), (), s32[]{:S(2)}) async-start(), calls=%async_computation.49 | async-start | bytes 5013504 | tf_op jit(solution)/shard_map/reduce_scatter | solution.py:418
  1016.8 519.0 %reduce-scatter.53.cloned.1.call-start = ((), (), s32[]{:S(2)}) async-start(), calls=%async_computation.42 | async-start | bytes 1253376 | tf_op jit(solution)/shard_map/reduce_scatter | solution.py:417
  1020.6 576.3 %reduce-scatter.71.cloned.1.call-start = ((), (), s32[]{:S(2)}) async-start(), calls=%async_computation.51 | async-start | bytes 1253376
  1026.8 631.2 %reduce-scatter.73.cloned.1.call-start = ((), (), s32[]{:S(2)}) async-start(), calls=%async_computation.52 | async-start | bytes 1253376
  1033.3 685.7 %reduce-scatter.75.cloned.1.call-start = ((), (), s32[]{:S(2)}) async-start(), calls=%async_computation.53 | async-start | bytes 1253376
  1039.3 758.5 %reduce-scatter.57.cloned.1.call-start = ((), (), s32[]{:S(2)}) async-start(), calls=%async_computation.44 | async-start | bytes 5013504 | tf_op jit(solution)/shard_map/reduce_scatter | solution.py:420
  1046.9 830.0 %reduce-scatter.55.cloned.1.call-start = ((), (), s32[]{:S(2)}) async-start(), calls=%async_computation.43 | async-start | bytes 5013504 | tf_op jit(solution)/shard_map/reduce_scatter | solution.py:418
  1095.8 48.0 %copy-start.8 = (bf16[512,768]{1,0:T(8,128)(2,1)S(1)}, bf16[512,768]{1,0:T(8,128)(2,1)}, u32[]{:S(2)}) copy-start(bf16[512,768]{1,0:T(8,128)(2,1)} %add_convert_fusion.4) | copy-start | bytes 2359300
  1095.8 48.0 %copy-start.27 = (bf16[512,768]{1,0:T(8,128)(2,1)S(1)}, bf16[512,768]{1,0:T(8,128)(2,1)}, u32[]{:S(2)}) copy-start(bf16[512,768]{1,0:T(8,128)(2,1)} %reduce-scatter.43.cloned.1.call-done) | copy-start | bytes 2359300
  1095.8 47.9 %copy-start.64 = (f32[768]{0:T(1024)S(1)}, f32[768]{0:T(1024)}, u32[]{:S(2)}) copy-start(f32[768]{0:T(1024)} %get-tuple-element.926) | copy-start | bytes 9220
  1095.8 47.9 %copy-start.74 = (f32[512]{0:T(512)S(1)}, f32[512]{0:T(512)}, u32[]{:S(2)}) copy-start(f32[512]{0:T(512)} %copy-done.73) | copy-start | bytes 6148
  1095.8 47.9 %copy-start.76 = (f32[768]{0:T(1024)S(1)}, f32[768]{0:T(1024)}, u32[]{:S(2)}) copy-start(f32[768]{0:T(1024)} %get-tuple-element.916) | copy-start | bytes 9220
  1095.8 47.9 %copy-start.92 = (f32[512]{0:T(512)S(1)}, f32[512]{0:T(512)}, u32[]{:S(2)}) copy-start(f32[512]{0:T(512)} %copy-done.91) | copy-start | bytes 6148
  (130 other events, 1229.9 us)
Sparse Core Ops, SparseCore 0:
  10.4 29.8 all-gather.12
  201.5 24.1 reduce-scatter.36
  327.4 24.5 reduce-scatter.38
  355.6 27.1 all-gather.20
  476.6 23.6 reduce-scatter.40
  599.3 24.5 reduce-scatter.42
  630.7 27.2 all-gather.28
  673.9 26.0 reduce-scatter.44
  708.2 27.2 all-gather.30
  823.4 27.2 all-gather.32
  864.1 26.0 reduce-scatter.48
Sparse Core Ops, SparseCore 1:
  204.2 40.1 all-gather.16
  247.1 28.5 all-gather.14
  278.1 42.7 all-gather.18
  479.8 40.3 all-gather.24
  521.8 25.5 all-gather.22
  550.0 42.7 all-gather.26
  791.1 25.9 reduce-scatter.46
  896.4 27.0 all-gather.34
  927.3 56.5 reduce-scatter.78
  987.5 55.6 reduce-scatter.76
  1045.4 25.0 reduce-scatter.50
  1074.6 57.9 reduce-scatter.64
  1136.6 57.1 reduce-scatter.58
  1198.0 57.0 reduce-scatter.60
  1259.3 56.9 reduce-scatter.62
  1320.7 74.4 reduce-scatter.68
  1400.0 74.4 reduce-scatter.66
  1478.7 57.0 reduce-scatter.52
  1539.8 56.9 reduce-scatter.70
  1601.0 56.9 reduce-scatter.72
  1662.1 56.9 reduce-scatter.74
  1723.4 74.3 reduce-scatter.56
  1802.5 74.3 reduce-scatter.54
where the time goes:
time: 1900 us; the launch traced here: 1880 us
  waiting for transfers between devices  1110 us (58%)
  blocking collectives  341 us (18%)
  matrix products  232 us (12%)
  local copies, waits for them, and re-layouts  97.6 us (5%)
  other arithmetic  57.2 us (3%)
  loops' own time  21.5 us (1%)
  between operations  19.6 us (1%)
    unnamed x39, waiting for transfers between devices  187 us
    unnamed x4, blocking collectives  173 us
    reduce_scatter x2, waiting for transfers between devices, local(): lax.psum_scatter(weight_terms[6], 'dp', scatter_dimension=0, tiled=True)  159 us
    reduce_scatter x2, waiting for transfers between devices, local(): lax.psum_scatter(weight_terms[8], 'dp', scatter_dimension=1, tiled=True)  158 us
    all_gather x4, waiting for transfers between devices, gather_grads(): return lax.all_gather(shard, 'tensor', axis=0, tiled=True)  106 us
    reduce_scatter x4, waiting for transfers between devices, sum_grads(): lax.psum_scatter(part_sums.astype(jnp.bfloat16), 'tensor', scatter_dimens...  78 us
    dot_general x12, matrix products, product(): return jnp.dot(first_op, second_op, preferred_element_type=jnp.float32)  74.5 us
    reduce_scatter x4, waiting for transfers between devices, sum_rows(): lax.psum_scatter(part_sums.astype(jnp.bfloat16), 'tensor', scatter_dimens...  71.1 us
  transfers between devices with their start and end apart: 34, of which 26 were waited for; matrix products, arithmetic and copies ran while one was open for 10% of the time, Pallas kernels for 0%

commit v1 on v0

v1 whole, which is shorter than its diff:
```python
import functools

import jax
import jax.numpy as jnp
from jax import lax
from jax.experimental import pallas as pl
from jax.experimental.pallas import tpu as pltpu
from jax.sharding import PartitionSpec as P

HEAD = 64
EPS = 1e-06
NEG = -1e30
WAVES = 6
NZ, NY, NC, NX = 4, 2, 2, 2
MESH = pl.DeviceIdType.MESH
BF = jnp.bfloat16
F32 = jnp.float32
AXES = ("dp", "tensor")


def place():
    dp = lax.axis_index("dp")
    t = lax.axis_index("tensor")
    return dp // 4, lax.rem(dp // 2, 2), lax.rem(dp, 2), t


def device(z, y, c, t):
    return {"dp": z * 4 + y * 2 + c, "tensor": t}


def greet(others):
    barrier = pltpu.get_barrier_semaphore()
    for other in others:
        pl.semaphore_signal(barrier, inc=1, device_id=other, device_id_type=MESH)
    pl.semaphore_wait(barrier, len(others))


def send(src, dst, sems, index, other):
    copy = pltpu.make_async_remote_copy(
        src_ref=src,
        dst_ref=dst,
        send_sem=sems[0].at[index],
        recv_sem=sems[1].at[index],
        device_id=other,
        device_id_type=MESH,
    )
    copy.start()
    return copy


def partners():
    z, y, c, t = place()
    core = device(z, y, 1 - c, t)
    over_x = device(z, y, c, 1 - t)
    over_y = device(z, 1 - y, c, t)
    over_z = [device(lax.rem(z + j, NZ), y, c, t) for j in range(1, NZ)]
    return core, over_x, over_y, over_z


def small_sum(src, dst, got, acc, sems):
    core, over_x, over_y, over_z = partners()
    now = src
    for step, other in enumerate((core, over_x, over_y)):
        send(now, got.at[step], sems, step, other).wait()
        acc[step] = now[...] + got[step]
        now = acc.at[step]
    copies = [send(now, got.at[3 + j], sems, 3 + j, other) for j, other in enumerate(over_z)]
    for copy in copies:
        copy.wait()
    dst[...] = now[...] + got[3] + got[4] + got[5]


def gather_kernel(shard, small, full, small_out, got, acc, s_send, s_recv, own_sem, b_send, b_recv):
    z, y, c, t = place()
    core, over_x, over_y, over_z = partners()
    greet([core, over_x, over_y] + over_z)
    half = shard.shape[2] // 2
    lo, hi = pl.ds(0, half), pl.ds(half, half)
    sems = (b_send, b_recv)
    owns, first, second, third, last = {}, {}, {}, {}, {}

    def start_first(k):
        owns[k] = pltpu.make_async_copy(shard.at[k], full.at[k, t, z, y, c], own_sem.at[k])
        owns[k].start()
        first[k] = [
            send(shard.at[k], full.at[k, t, z, y, c], sems, (k, j), other)
            for j, other in enumerate(over_z)
        ]

    def start_second(k):
        owns[k].wait()
        for copy in first[k]:
            copy.wait()
        a = full.at[k, t, :, y, c, :, lo]
        b = full.at[k, t, :, y, c, :, hi]
        second[k] = [send(a, a, sems, (k, 3), over_y), send(b, b, sems, (k, 4), over_x)]

    def start_third(k):
        for copy in second[k]:
            copy.wait()
        a = full.at[k, t, :, :, c, :, lo]
        b = full.at[k, :, :, y, c, :, hi]
        third[k] = [send(a, a, sems, (k, 5), over_x), send(b, b, sems, (k, 6), over_y)]

    def start_last(k):
        for copy in third[k]:
            copy.wait()
        a = full.at[k, :, :, :, c]
        last[k] = send(a, a, sems, (k, 7), core)

    start_first(0)
    start_first(1)
    small_sum(small, small_out, got, acc, (s_send, s_recv))
    for step in range(WAVES + 2):
        if step < WAVES:
            start_second(step)
            if step + 2 < WAVES:
                start_first(step + 2)
        if 0 <= step - 1 < WAVES:
            start_third(step - 1)
        if 0 <= step - 2 < WAVES:
            start_last(step - 2)
    for k in range(WAVES):
        last[k].wait()


def gather_all(shard, small):
    waves, rows, cols = shard.shape
    dma = pltpu.SemaphoreType.DMA
    any_spec = pl.BlockSpec(memory_space=pl.ANY)
    vmem = pl.BlockSpec(memory_space=pltpu.VMEM)
    full, small_out = pl.pallas_call(
        gather_kernel,
        out_shape=(
            jax.ShapeDtypeStruct((waves, NX, NZ, NY, NC, rows, cols), BF),
            jax.ShapeDtypeStruct(small.shape, F32),
        ),
        in_specs=[any_spec, vmem],
        out_specs=(any_spec, vmem),
        scratch_shapes=[
            pltpu.VMEM((6,) + small.shape, F32),
            pltpu.VMEM((3,) + small.shape, F32),
            dma((6,)),
            dma((6,)),
            dma((waves,)),
            dma((waves, 8)),
            dma((waves, 8)),
        ],
        name="gather_all",
        compiler_params=pltpu.CompilerParams(
            collective_id=0, has_side_effects=True, vmem_limit_bytes=32 << 20
        ),
    )(shard, small)
    return full.reshape(waves, NX, NZ * NY * NC * rows, cols), small_out


def reduce_kernel(*refs):
    parts, refs = refs[:WAVES], refs[WAVES:]
    small, out, small_out, own, rc, r2a, r2b, r3a, r3b, r4, got, acc, s_send, s_recv, own_sem, b_send, b_recv = refs
    z, y, c, t = place()
    core, over_x, over_y, over_z = partners()
    greet([core, over_x, over_y] + over_z)
    half = out.shape[2] // 2
    lo, hi = pl.ds(0, half), pl.ds(half, half)
    sems = (b_send, b_recv)
    local, first, second, third, last = {}, {}, {}, {}, {}

    def start_first(k):
        local[k] = pltpu.make_async_copy(parts[k].at[:, :, :, c], own.at[k % 2], own_sem.at[k % 2])
        local[k].start()
        first[k] = send(parts[k].at[:, :, :, 1 - c], rc.at[k], sems, (k, 0), core)

    def start_second(k):
        local[k].wait()
        first[k].wait()

        @pl.loop(0, NZ)
        def _(i):
            for a in range(NX):
                for b in range(NY):
                    rc[k, a, i, b] = rc[k, a, i, b] + own[k % 2, a, i, b]

        second[k] = [
            send(rc.at[k, 1 - t, :, :, :, lo], r2a.at[k], sems, (k, 1), over_x),
            send(rc.at[k, :, :, 1 - y, :, hi], r2b.at[k], sems, (k, 2), over_y),
        ]

    def start_third(k):
        for copy in second[k]:
            copy.wait()

        @pl.loop(0, NZ)
        def _(i):
            for b in range(2):
                rc[k, t, i, b, :, lo] = rc[k, t, i, b, :, lo] + r2a[k, i, b]
                rc[k, b, i, y, :, hi] = rc[k, b, i, y, :, hi] + r2b[k, b, i]

        third[k] = [
            send(rc.at[k, t, :, 1 - y, :, lo], r3a.at[k], sems, (k, 3), over_y),
            send(rc.at[k, 1 - t, :, y, :, hi], r3b.at[k], sems, (k, 4), over_x),
        ]

    def start_last(k):
        for copy in third[k]:
            copy.wait()

        @pl.loop(0, NZ)
        def _(i):
            rc[k, t, i, y, :, lo] = rc[k, t, i, y, :, lo] + r3a[k, i]
            rc[k, t, i, y, :, hi] = rc[k, t, i, y, :, hi] + r3b[k, i]

        last[k] = [
            send(rc.at[k, t, lax.rem(z + j + 1, NZ), y], r4.at[k, j], sems, (k, 5 + j), other)
            for j, other in enumerate(over_z)
        ]

    def finish(k):
        for copy in last[k]:
            copy.wait()
        total = rc[k, t, z, y].astype(F32)
        for j in range(3):
            total = total + r4[k, j].astype(F32)
        out[k] = total

    start_first(0)
    for step in range(WAVES + 3):
        if step < WAVES:
            if step + 1 < WAVES:
                start_first(step + 1)
            start_second(step)
        if 0 <= step - 1 < WAVES:
            start_third(step - 1)
        if 0 <= step - 2 < WAVES:
            start_last(step - 2)
        if 0 <= step - 3 < WAVES:
            finish(step - 3)
    small_sum(small, small_out, got, acc, (s_send, s_recv))


def reduce_all(parts, small):
    _, width, cols = parts[0].shape
    rows = width // (NZ * NY * NC)
    shaped = [part.reshape(NX, NZ, NY, NC, rows, cols) for part in parts]
    dma = pltpu.SemaphoreType.DMA
    any_spec = pl.BlockSpec(memory_space=pl.ANY)
    vmem = pl.BlockSpec(memory_space=pltpu.VMEM)
    return pl.pallas_call(
        reduce_kernel,
        out_shape=(
            jax.ShapeDtypeStruct((WAVES, rows, cols), F32),
            jax.ShapeDtypeStruct(small.shape, F32),
        ),
        in_specs=[any_spec] * WAVES + [vmem],
        out_specs=(vmem, vmem),
        scratch_shapes=[
            pltpu.VMEM((2, NX, NZ, NY, rows, cols), BF),
            pltpu.VMEM((WAVES, NX, NZ, NY, rows, cols), BF),
            pltpu.VMEM((WAVES, NZ, NY, rows, cols // 2), BF),
            pltpu.VMEM((WAVES, NX, NZ, rows, cols // 2), BF),
            pltpu.VMEM((WAVES, NZ, rows, cols // 2), BF),
            pltpu.VMEM((WAVES, NZ, rows, cols // 2), BF),
            pltpu.VMEM((WAVES, 3, rows, cols), BF),
            pltpu.VMEM((6,) + small.shape, F32),
            pltpu.VMEM((3,) + small.shape, F32),
            dma((6,)),
            dma((6,)),
            dma((2,)),
            dma((WAVES, 8)),
            dma((WAVES, 8)),
        ],
        name="reduce_all",
        compiler_params=pltpu.CompilerParams(
            collective_id=1, has_side_effects=True, vmem_limit_bytes=56 << 20
        ),
    )(*shaped, small)


def gather_plain(shard, small):
    rows = lax.all_gather(shard, "dp", axis=1, tiled=True)
    full = lax.all_gather(rows, "tensor", axis=1, tiled=False)
    return full, lax.psum(small, AXES)


def reduce_plain(parts, small):
    outs = []
    for part in parts:
        mine = lax.psum_scatter(part.astype(F32), "tensor", scatter_dimension=0, tiled=True)[0]
        outs.append(lax.psum_scatter(mine, "dp", scatter_dimension=0, tiled=True))
    return jnp.stack(outs), lax.psum(small, AXES)


def layer_norm(residual, gain, shift):
    average = jnp.mean(residual, axis=-1, keepdims=True)
    centred = residual - average
    variance = jnp.mean(centred * centred, axis=-1, keepdims=True)
    return centred * lax.rsqrt(variance + EPS) * gain + shift


def gelu_exact(value):
    return jax.nn.gelu(value, approximate=False)


def ein(spec, a, b):
    return jnp.einsum(spec, a, b, preferred_element_type=F32)


def heads_of(value):
    return value.reshape(value.shape[0], value.shape[1], value.shape[2] // HEAD, HEAD)


def scores_of(queries, keys, valid):
    raw = ein("tqhd,tkhd->thqk", heads_of(queries), heads_of(keys)) * (HEAD**-0.5)
    return jnp.where(valid, raw, NEG)


def layer_forward(rows, groups, small, valid):
    w_attn, w_up, w_down = groups
    width = rows.shape[1]
    half = width // 2
    bq = small[0].reshape(2, 1, half)
    bv = small[1].reshape(2, 1, half)
    bo, g1, s1, bd, g2, s2 = (small[i][None, :] for i in range(2, 8))
    bu = small[8:].reshape(2, 1, -1)
    qkv = ein("nd,tdc->tnc", rows, w_attn[:, :, : 3 * half])
    queries = (qkv[:, :, :half] + bq).astype(BF)
    keys = qkv[:, :, half : 2 * half].astype(BF)
    values = (qkv[:, :, 2 * half :] + bv).astype(BF)
    scores = scores_of(queries, keys, valid)
    row_max = jnp.max(scores, axis=-1, keepdims=True)
    exponent = jnp.exp(scores - row_max)
    total = jnp.sum(exponent, axis=-1, keepdims=True)
    probs = (exponent / total).astype(BF)
    attended = ein("thqk,tkhd->tqhd", probs, heads_of(values)).astype(BF).reshape(queries.shape)
    log_sums = row_max + jnp.log(total)
    branch = ein("tnc,tdc->nd", attended, w_attn[:, :, 3 * half :])
    resid_one = rows.astype(F32) + branch + bo
    hidden = layer_norm(resid_one, g1, s1).astype(BF)
    upward = ein("nd,tdc->tnc", hidden, w_up) + bu
    active = gelu_exact(upward).astype(BF)
    resid_two = hidden.astype(F32) + ein("tnc,tdc->nd", active, w_down) + bd
    result = layer_norm(resid_two, g2, s2)
    saved = (rows, queries, keys, values, attended, log_sums, resid_one, hidden, upward, active, resid_two)
    return result, saved


def layer_backward(d_result, groups, small, saved, valid):
    w_attn, w_up, w_down = groups
    rows, queries, keys, values, attended, log_sums, resid_one, hidden, upward, active, resid_two = saved
    half = rows.shape[1] // 2
    g1, s1, g2, s2 = (small[i] for i in (3, 4, 6, 7))
    _, norm_two_back = jax.vjp(layer_norm, resid_two, g2, s2)
    d_resid_two, d_g2, d_s2 = norm_two_back(d_result)
    d_down = d_resid_two.astype(BF)
    gw_down = ein("nd,tnc->tdc", d_down, active).astype(BF)
    _, gelu_back = jax.vjp(gelu_exact, upward)
    d_up = gelu_back(ein("nd,tdc->tnc", d_down, w_down))[0].astype(BF)
    gw_up = ein("nd,tnc->tdc", hidden, d_up).astype(BF)
    d_bu = jnp.sum(d_up, axis=1, dtype=F32).reshape(4, -1)
    d_hidden = d_resid_two + ein("tnc,tdc->nd", d_up, w_up)
    _, norm_one_back = jax.vjp(layer_norm, resid_one, g1, s1)
    d_resid_one, d_g1, d_s1 = norm_one_back(d_hidden)
    d_branch = d_resid_one.astype(BF)
    gw_out = ein("nd,tnc->tdc", d_branch, attended)
    d_attended = ein("nd,tdc->tnc", d_branch, w_attn[:, :, 3 * half :]).astype(BF)
    probs = jnp.exp(scores_of(queries, keys, valid) - log_sums)
    d_probs = ein("tqhd,tkhd->thqk", heads_of(d_attended), heads_of(values))
    d_scores = (probs * (d_probs - jnp.sum(probs * d_probs, axis=-1, keepdims=True))).astype(BF)
    scale = HEAD**-0.5
    d_queries = (ein("thqk,tkhd->tqhd", d_scores, heads_of(keys)) * scale).astype(BF).reshape(queries.shape)
    d_keys = (ein("thqk,tqhd->tkhd", d_scores, heads_of(queries)) * scale).astype(BF).reshape(queries.shape)
    d_values = ein("thqk,tqhd->tkhd", probs.astype(BF), heads_of(d_attended)).astype(BF).reshape(queries.shape)
    d_qkv = jnp.concatenate([d_queries, d_keys, d_values], axis=2)
    gw_attn = jnp.concatenate([ein("nd,tnc->tdc", rows, d_qkv), gw_out], axis=2).astype(BF)
    d_input = d_resid_one + ein("tnc,tdc->nd", d_qkv, w_attn[:, :, : 3 * half])
    d_small = jnp.concatenate(
        [
            jnp.sum(d_queries, axis=1, dtype=F32).reshape(1, -1),
            jnp.sum(d_values, axis=1, dtype=F32).reshape(1, -1),
            jnp.sum(d_resid_one, axis=0)[None],
            d_g1[None],
            d_s1[None],
            jnp.sum(d_resid_two, axis=0)[None],
            d_g2[None],
            d_s2[None],
            d_bu,
        ],
        axis=0,
    )
    return d_input, (gw_attn, gw_up, gw_down), d_small


def pack_weights(args):
    query_w, _, key_w, value_w, _, out_w, _, _, _, up_w, _, down_w = args[:12]
    return jnp.stack([jnp.concatenate([query_w, key_w, value_w, out_w.T], axis=1), up_w, down_w.T])


def spread(values, where, count):
    n, m = values.shape
    block = jnp.arange(m * count) // m
    return jnp.where(block[None, :] == where, jnp.tile(values.astype(F32), (1, count)), 0.0)


def pack_small(args, dp, n_dp, t):
    query_b, value_b, up_b = args[1], args[4], args[10]
    biases = spread(jnp.concatenate([query_b, value_b], axis=0), t * n_dp + dp, 2 * n_dp)
    norms = spread(jnp.stack([args[6], args[7], args[8], args[12], args[13], args[14]]), 2 * dp + t, 2 * n_dp)
    ups = spread(up_b, t * n_dp + dp, 2 * n_dp).reshape(4, -1)
    return jnp.concatenate([biases, norms, ups], axis=0)


def take(values, where, count):
    n, width = values.shape
    m = width // count
    return lax.dynamic_slice_in_dim(values, where * m, m, 1)


def local(n_dp, fast, *args):
    inputs, lengths, grad_out = args[0], args[1], args[-1]
    teacher, student = args[2:17], args[17:32]
    dp, t = lax.axis_index("dp"), lax.axis_index("tensor")
    seq_len = inputs.shape[0]
    width = inputs.shape[1]
    half = width // 2
    my_length = lax.dynamic_index_in_dim(lengths, t, 0, keepdims=False)
    inside = jnp.arange(seq_len) < my_length
    row_mask = inside.astype(F32)[:, None]
    valid = inside[None, None, None, :]
    shard = jnp.concatenate([pack_weights(teacher), pack_weights(student)], axis=0)
    small = jnp.concatenate([pack_small(teacher, dp, n_dp, t), pack_small(student, dp, n_dp, t)], axis=0)
    full, small = (gather_all if fast else gather_plain)(shard, small)
    groups = [tuple(full[3 * layer + i] for i in range(3)) for layer in range(2)]
    smalls = [small[:12], small[12:]]
    result, kept_t = layer_forward(inputs, groups[0], smalls[0], valid)
    result, kept_s = layer_forward(result.astype(BF), groups[1], smalls[1], valid)
    activations = (result * row_mask).astype(BF)
    d_current = grad_out.astype(F32) * row_mask
    d_current, parts_s, small_s = layer_backward(d_current, groups[1], smalls[1], kept_s, valid)
    d_current, parts_t, small_t = layer_backward(d_current, groups[0], smalls[0], kept_t, valid)
    order = (parts_s[2], parts_s[1], parts_s[0], parts_t[2], parts_t[1], parts_t[0])
    sums, small_sums = (reduce_all if fast else reduce_plain)(order, jnp.concatenate([small_t, small_s], axis=0))
    outs = [activations, d_current]
    for layer in range(2):
        base = 3 * (1 - layer)
        g_down, g_up, g_attn = sums[base], sums[base + 1], sums[base + 2]
        part = small_sums[12 * layer : 12 * layer + 12]
        biases = take(part[0:2], t * n_dp + dp, 2 * n_dp)
        norms = take(part[2:8], 2 * dp + t, 2 * n_dp)
        ups = take(part[8:12].reshape(1, -1), t * n_dp + dp, 2 * n_dp)
        outs += [
            g_attn[:, :half],
            biases[0:1],
            g_attn[:, half : 2 * half],
            g_attn[:, 2 * half : 3 * half],
            biases[1:2],
            g_attn[:, 3 * half :].T,
            norms[0],
            norms[1],
            norms[2],
            g_up,
            ups,
            g_down.T,
            norms[3],
            norms[4],
            norms[5],
        ]
    return tuple(outs)


def solution(mesh):
    n_dp = mesh.shape["dp"]
    fast = n_dp == NZ * NY * NC and mesh.shape["tensor"] == NX
    row = P(AXES, None)
    vec = P(AXES)
    cut_in, cut_out = P("dp", "tensor"), P("tensor", "dp")
    layer = (cut_in, cut_out, cut_in, cut_in, cut_out, cut_out, vec, vec, vec, cut_in, cut_out, cut_out, vec, vec, vec)
    return jax.shard_map(
        functools.partial(local, n_dp, fast),
        mesh=mesh,
        in_specs=(row, P("dp")) + layer + layer + (row,),
        out_specs=(row, row) + layer + layer,
        check_vma=False,
    )
```

time: 1900 us -> 629 us (0.33)
  waiting for transfers between devices: 1110 us -> 0 us
  blocking collectives: 341 us -> 0 us
  Pallas kernels: 0 us -> 319 us
  matrix products: 232 us -> 186 us
  local copies, waits for them, and re-layouts: 97.6 us -> 75.3 us
  loops' own time: 21.5 us -> 0 us
    reduce_scatter x17 -> x0, waiting for transfers between devices: 698 us -> none  [the longest x2 159 us: local(): lax.psum_scatter(weight_terms[6], 'dp', scatter_dimension=0, tiled=True)]
    pallas_call x0 -> x2, Pallas kernels: none -> 319 us  [the longest x1 162 us: reduce_all(): pl.pallas_call(reduce_kernel, out_shape=(jax.ShapeDtypeStruct((WAVES, row...]
    all_gather x12 -> x0, waiting for transfers between devices: 227 us -> none  [the longest x4 106 us: gather_grads(): return lax.all_gather(shard, 'tensor', axis=0, tiled=True)]
    unnamed x39 -> x0, waiting for transfers between devices: 187 us -> none
    unnamed x4 -> x0, blocking collectives: 173 us -> none
    all_gather x8 -> x0, blocking collectives: 168 us -> none  [the longest x2 42.4 us: local(): lax.all_gather(mats[3], 'dp', axis=0, tiled=True)]
    dot_general x64 -> x36, matrix products: 232 us -> 186 us  [ein(): return jnp.einsum(spec, a, b, preferred_element_type=F32)]
    unnamed x294 -> x150, local copies, waits for them, and re-layouts: 43.3 us -> 11.5 us
  transfers between devices with their start and end apart: 34 -> 0, of which waited for: 26 -> 0; matrix products, arithmetic and copies ran while one was open for 10% -> 0% of each run, Pallas kernels for 0% -> 0%
where the time goes in v1:
time: 629 us; the launch traced here: 624 us
  Pallas kernels  319 us (51%)
  matrix products  186 us (30%)
  local copies, waits for them, and re-layouts  75.3 us (12%)
  other arithmetic  41.8 us (7%)
    dot_general x36, matrix products, ein(): return jnp.einsum(spec, a, b, preferred_element_type=F32)  186 us
    pallas_call x1, Pallas kernels, reduce_all(): pl.pallas_call(reduce_kernel, out_shape=(jax.ShapeDtypeStruct((WAVES, row...  162 us
    pallas_call x1, Pallas kernels, gather_all(): pl.pallas_call(gather_kernel, out_shape=(jax.ShapeDtypeStruct((waves, NX,...  157 us
    slice x1, local copies, waits for them, and re-layouts, local(): full[3 * layer + i]  21.1 us
    convert_element_type x2, other arithmetic, layer_backward(): (probs * (d_probs - jnp.sum(probs * d_probs, axis=-1, keepdims=True))).as...  14.1 us

profile of v1, /device:TPU:0, one launch (start us, length us, event | category | flops | bytes accessed | tf_op | source)
XLA Modules:
  0.0 623.7 jit_solution(6637581132420407267)
XLA Ops:
  13.6 157.0 %gather_all.1 = (bf16[6,2,4,2,2,48,1536]{6,5,4,3,2,1,0:T(8,128)(2,1)}, f32[24,768]{1,0:T(8,128)S(1)}) custom-call(bf16[6,48,1536]{2,1,0:T(8,128)(2,1)S(1)} %bitcast_dynamic-update-slice_fusion.shard, f32[24,768]{1,0:T(8,128)S(1)} %concatenate.58.small), custom_call_target="tpu_custom_call" | custom-call | tf_op jit(solution)/shard_map/gather_all/pallas_call | solution.py:132
  170.6 21.1 %fusion.134 = (bf16[1,2,4,2,2,48,1536]{6,5,4,3,2,1,0:T(8,128)(2,1)}, bf16[1,2,4,2,2,48,1536]{6,5,4,3,2,1,0:T(8,128)(2,1)}, bf16[1,2,4,2,2,48,1536]{6,5,4,3,2,1,0...) fusion(bf16[6,2,4,2,2,48,1536]{6,5,4,3,2,1,0:T(8,128)(2,1)} %ge, ...), kind=kLoop, calls=%fused_computation.302 | loop fusion | bytes 56623104 | tf_op jit(solution)/shard_map/slice | solution.py:431
  192.4 4.1 convolution_bitcast_fusion.1
  197.8 3.0 fusion.140
  203.4 3.2 copy-done
  206.6 3.7 fusion.85
  210.4 2.5 fusion.141
  213.9 27.8 %fusion.27 = (bf16[2,512,1536]{2,1,0:T(8,128)(2,1)S(1)}, f32[2,512,1536]{2,1,0:T(8,128)}, f32[2,1536,512]{1,2,0:T(8,128)}) fusion(f32[2,1536]{1,0:T(2,128)S(1)} %add.290, bf16[2,768,1536]{2,1,0:T(8,128)(2,1)S(1)} %bitcast.455, f32[512,768]{1,0:T(8,128)S(1)} %get-tuple-element.136, f32[768]{0:T(1024)S(1)} %get-tuple-element.63, ...), kind=kOutput, calls=%fused_computation.53 | convolution fusion | flops 2521694208 | bytes 22042624 | tf_op jit(solution)/shard_map/nd,tdc->tnc/dot_general | solution.py:304
  241.8 2.8 fusion.142
  245.0 2.3 convolution_bitcast_fusion
  247.7 3.0 fusion.143
  252.6 2.6 copy-done.1
  255.2 2.8 fusion.84
  258.0 2.8 fusion.144
  261.2 19.7 %fusion.25 = (bf16[2,512,1536]{2,1,0:T(8,128)(2,1)S(1)}, f32[2,512,1536]{2,1,0:T(8,128)}, f32[2,1536,512]{1,2,0:T(8,128)}) fusion(f32[2,1536]{1,0:T(2,128)S(1)} %add.315, bf16[2,768,1536]{2,1,0:T(8,128)(2,1)} %bitcast.469, f32[512,768]{1,0:T(8,128)S(1)} %get-tuple-element.143, f32[768]{0:T(1024)S(1)} %get-tuple-element.55, f32[768]{0:T(1024)S(1)} %get-tuple-element.56, ...), kind=kOutput, calls=%fused_computation.46 | convolution fusion | flops 2521694208 | bytes 22042624 | tf_op jit(solution)/shard_map/nd,tdc->tnc/dot_general | solution.py:304
  281.0 2.8 fusion.145
  287.4 7.1 %convert_reduce_fusion = (f32[2,1536]{1,0:T(2,128)S(1)}, bf16[2,512,1536]{2,1,0:T(8,128)(2,1)S(1)}) fusion(f32[2,512,1536]{2,1,0:T(8,128)S(1)} %bitcast.520, bf16[2,768,1536]{2,1,0:T(8,128)(2,1)S(1)} %bitcast.476, f32[512,768]{1,0:T(8,128)S(1)} %get-tuple-element.75, f32[512]{0:T(512)S(1)} %negate_multiply_fusion.5, ...), kind=kOutput, calls=%fused_computation.54 | convolution fusion | flops 2443441152 | bytes 22046720 | tf_op jit(solution)/shard_map/nd,tdc->tnc/dot_general | solution.py:304
  294.6 4.0 multiply_reduce_fusion.3
  299.3 2.8 fusion.130
  302.1 4.7 convolution_convert_fusion.4
  308.3 4.5 convolution_convert_fusion.5
  313.4 1.9 fusion.76
  315.3 2.4 copy.120
  317.6 2.7 convolution_convert_fusion.9
  320.3 7.8 %convert_reduce_fusion.2 = (f32[2,6,64]{2,1,0:T(8,128)S(1)}, bf16[2,6,64,512]{3,2,1,0:T(8,128)(2,1)}) fusion(bf16[2,512,6,64]{1,3,2,0:T(8,128)(2,1)S(1)} %bitcast.489, f32[2,6,512,512]{2,3,1,0:T(8,128)} %copy-done.1, f32[2,6,512]{2,1,0:T(8,128)S(1)} %log_add_fusion.1), kind=kOutput, calls=%fused_computation.132 | convolution fusion | flops 410123520 | bytes 14183424 | tf_op jit(solution)/shard_map/thqk,tqhd->tkhd/dot_general | solution.py:304
  328.8 2.3 copy.107
  331.1 7.6 %multiply_reduce_fusion.1 = (f32[2,6,512]{2,1,0:T(8,128)S(1)}, f32[2,6,512,512]{2,3,1,0:T(8,128)S(1)}) fusion(f32[2,6,512,512]{2,3,1,0:T(8,128)} %copy-done.1, f32[2,6,512]{2,1,0:T(8,128)S(1)} %log_add_fusion.1, bf16[2,512,6,64]{1,3,2,0:T(8,128)(2,1)} %bitcast.490, bf16[2,512,6,64]{1,3,2,0:T(8,128)(2,1)} %bitcast.488), kind=kOutput, calls=%fused_computation.4 | convolution fusion | flops 412084224 | bytes 26787840 | tf_op jit(solution)/shard_map/tqhd,tkhd->thqk/dot_general | solution.py:304
  338.7 7.1 %multiply_convert_fusion.1 = bf16[2,6,512,512]{2,3,1,0:T(8,128)(2,1)S(1)} fusion(f32[2,6,512,512]{2,3,1,0:T(8,128)S(1)} %get-tuple-element.149, f32[2,6,512,512]{2,3,1,0:T(8,128)} %copy-done.1, f32[2,6,512]{2,1,0:T(8,128)S(1)} %get-tuple-element.148, f32[2,6,512]{2,1,0:T(8,128)S(1)} %log_add_fusion.1), kind=kLoop, calls=%fused_computation.3 | loop fusion | flops 12582912 | bytes 31506432 | tf_op jit(solution)/shard_map/convert_element_type | solution.py:367
  345.8 2.9 multiply_convert_fusion.4
  352.4 5.1 multiply_reduce_fusion.4
  358.8 4.0 convolution_convert_fusion.3
  362.8 9.2 %convert_reduce_fusion.1 = (f32[2,1536]{1,0:T(2,128)S(1)}, bf16[2,512,1536]{2,1,0:T(8,128)(2,1)S(1)}) fusion(f32[2,512,1536]{2,1,0:T(8,128)} %get-tuple-element.79, bf16[2,768,1536]{2,1,0:T(8,128)(2,1)} %bitcast.459, f32[512,768]{1,0:T(8,128)S(1)} %get-tuple-element.71, f32[512]{0:T(512)S(1)} %negate_multiply_fusion.3, ...), kind=kOutput, calls=%fused_computation.55 | convolution fusion | flops 2443441152 | bytes 22046720 | tf_op jit(solution)/shard_map/nd,tdc->tnc/dot_general | solution.py:304
  372.2 4.0 multiply_reduce_fusion.5
  377.4 4.8 pad_maximum_fusion.refs_2_
  384.2 4.6 convolution_convert_fusion.1
  390.9 4.6 convolution_convert_fusion.2
  399.7 2.2 convolution_convert_fusion.8
  401.9 8.4 %convert_reduce_fusion.4 = (f32[2,6,64]{2,1,0:T(8,128)}, bf16[2,6,64,512]{3,2,1,0:T(8,128)(2,1)}) fusion(bf16[2,512,6,64]{1,3,2,0:T(8,128)(2,1)S(1)} %bitcast.491, f32[2,6,512,512]{2,3,1,0:T(8,128)} %copy-done, f32[2,6,512]{2,1,0:T(8,128)} %log_add_fusion), kind=kOutput, calls=%fused_computation.136 | convolution fusion | flops 410123520 | bytes 14183424 | tf_op jit(solution)/shard_map/thqk,tqhd->tkhd/dot_general | solution.py:304
  411.6 2.3 copy.115
  414.0 7.3 %multiply_reduce_fusion = (f32[2,6,512]{2,1,0:T(8,128)S(1)}, f32[2,6,512,512]{2,3,1,0:T(8,128)S(1)}) fusion(f32[2,6,512,512]{2,3,1,0:T(8,128)} %copy-done, f32[2,6,512]{2,1,0:T(8,128)} %log_add_fusion, bf16[2,512,6,64]{1,3,2,0:T(8,128)(2,1)} %bitcast.492, bf16[2,512,6,64]{1,3,2,0:T(8,128)(2,1)S(1)} %bitcast.486), kind=kOutput, calls=%fused_computation.1 | convolution fusion | flops 412084224 | bytes 26787840 | tf_op jit(solution)/shard_map/tqhd,tkhd->thqk/dot_general | solution.py:304
  421.3 7.1 %multiply_convert_fusion = bf16[2,6,512,512]{2,3,1,0:T(8,128)(2,1)S(1)} fusion(f32[2,6,512,512]{2,3,1,0:T(8,128)S(1)} %get-tuple-element.153, f32[2,6,512,512]{2,3,1,0:T(8,128)} %copy-done, f32[2,6,512]{2,1,0:T(8,128)S(1)} %get-tuple-element.152, f32[2,6,512]{2,1,0:T(8,128)S(1)} %copy-done.25), kind=kLoop, calls=%fused_computation | loop fusion | flops 12582912 | bytes 31506432 | tf_op jit(solution)/shard_map/convert_element_type | solution.py:367
  428.3 2.9 multiply_convert_fusion.2
  434.3 4.1 concatenate.67.refs_6_
  441.2 5.8 bitcast_add_fusion
  447.0 2.1 convolution_convert_fusion
  449.1 2.9 pad_maximum_fusion.1.refs_5_
  451.9 161.7 %reduce_all.1 = (f32[6,48,1536]{2,1,0:T(8,128)}, f32[24,768]{1,0:T(8,128)}) custom-call(bf16[2,4,2,2,48,1536]{5,4,3,2,1,0:T(8,128)(2,1)} %bitcast.480, bf16[2,4,2,2,48,1536]{5,4,3,2,1,0:T(8,128)(2,1)} %bitcast.479, bf16[2,4,2,2,48,1536]{5,4,3,2,1,0:T(8,128)(2,1)} %pad_maximum_fusion.refs_2_, bf16[2,4,2,2,48,1536]{5,4,3,2,1,0:T(8,128)(2,1)} %bitcast.482, ...), custom_call_target="tpu_custom_call" | custom-call | tf_op jit(solution)/shard_map/reduce_all/pallas_call | solution.py:247
  613.7 2.5 slice_bitcast_fusion
  (268 shorter events, 56.9 us)
Async XLA Ops:
  170.6 21.8 %copy-start.43 = (bf16[512,768]{1,0:T(8,128)(2,1)S(1)}, bf16[512,768]{1,0:T(8,128)(2,1)}, u32[]{:S(2)}) copy-start(bf16[512,768]{1,0:T(8,128)(2,1)} %param.33) | copy-start | bytes 2359300
  192.3 49.4 %copy-start.32 = (f32[768]{0:T(1024)}, f32[768]{0:T(1024)S(1)}, u32[]{:S(2)}) copy-start(f32[768]{0:T(1024)S(1)} %get-tuple-element.64) | copy-start | bytes 9220
  192.3 49.4 %copy-start.40 = (f32[768]{0:T(1024)}, f32[768]{0:T(1024)S(1)}, u32[]{:S(2)}) copy-start(f32[768]{0:T(1024)S(1)} %get-tuple-element.63) | copy-start | bytes 9220
  192.4 21.4 %copy-start.35 = (f32[2,1536]{1,0:T(2,128)}, f32[2,1536]{1,0:T(2,128)S(1)}, u32[]{:S(2)}) copy-start(f32[2,1536]{1,0:T(2,128)S(1)} %add.290) | copy-start | bytes 36868
  200.9 5.7 copy-start
  200.9 12.9 %slice-start = ((s8[4718592]{0:T(1024)(128)(4,1)}), s8[4194304]{0:T(1024)(128)(4,1)S(1)}, s32[]{:S(2)}) async-start(s8[4718592]{0:T(1024)(128)(4,1)} %bitcast.453), calls=%async_computation | async-start | bytes 8388608
  206.6 7.2 %slice-start.1 = ((s8[4718592]{0:T(1024)(128)(4,1)}), s8[524288]{0:T(1024)(128)(4,1)S(1)}, s32[]{:S(2)}) async-start(s8[4718592]{0:T(1024)(128)(4,1)} %bitcast.453), calls=%async_computation.1 | async-start | bytes 1048576
  210.3 31.4 %copy-start.46 = (bf16[2,6,64,512]{3,2,1,0:T(8,128)(2,1)}, bf16[2,6,64,512]{3,2,1,0:T(8,128)(2,1)S(1)}, u32[]{:S(2)}) copy-start(bf16[2,6,64,512]{3,2,1,0:T(8,128)(2,1)S(1)} %fusion.85) | copy-start | bytes 2359300
  210.3 31.4 %slice-start.4 = ((s8[4718592]{0:T(1024)(128)(4,1)}), s8[4194304]{0:T(1024)(128)(4,1)S(1)}, s32[]{:S(2)}) async-start(s8[4718592]{0:T(1024)(128)(4,1)} %bitcast.460), calls=%async_computation.4 | async-start | bytes 8388608
  210.4 34.6 %slice-start.6 = ((s8[4718592]{0:T(1024)(128)(4,1)}), s8[4194304]{0:T(1024)(128)(4,1)S(1)}, s32[]{:S(2)}) async-start(s8[4718592]{0:T(1024)(128)(4,1)} %bitcast.466), calls=%async_computation.6 | async-start | bytes 8388608
  212.9 28.8 %copy-start.6 = (f32[512,768]{1,0:T(8,128)}, f32[512,768]{1,0:T(8,128)S(1)}, u32[]{:S(2)}) copy-start(f32[512,768]{1,0:T(8,128)S(1)} %get-tuple-element.136) | copy-start | bytes 4718596
  212.9 28.8 %copy-start.27 = (f32[512]{0:T(512)}, f32[512]{0:T(512)S(1)}, u32[]{:S(2)}) copy-start(f32[512]{0:T(512)S(1)} %broadcast_multiply_fusion.3) | copy-start | bytes 6148
  213.8 27.9 %copy-start.37 = (f32[512]{0:T(512)}, f32[512]{0:T(512)S(1)}, u32[]{:S(2)}) copy-start(f32[512]{0:T(512)S(1)} %fusion.119) | copy-start | bytes 6148
  213.8 27.9 %slice-start.5 = ((s8[4718592]{0:T(1024)(128)(4,1)}), s8[524288]{0:T(1024)(128)(4,1)S(1)}, s32[]{:S(2)}) async-start(s8[4718592]{0:T(1024)(128)(4,1)} %bitcast.460), calls=%async_computation.5 | async-start | bytes 1048576
  213.8 31.1 %slice-start.7 = ((s8[4718592]{0:T(1024)(128)(4,1)}), s8[524288]{0:T(1024)(128)(4,1)S(1)}, s32[]{:S(2)}) async-start(s8[4718592]{0:T(1024)(128)(4,1)} %bitcast.466), calls=%async_computation.7 | async-start | bytes 1048576
  258.0 22.9 %copy-start.48 = (bf16[2,6,64,512]{3,2,1,0:T(8,128)(2,1)}, bf16[2,6,64,512]{3,2,1,0:T(8,128)(2,1)S(1)}, u32[]{:S(2)}) copy-start(bf16[2,6,64,512]{3,2,1,0:T(8,128)(2,1)S(1)} %fusion.84) | copy-start | bytes 2359300
  258.0 22.9 %slice-start.10 = ((s8[4718592]{0:T(1024)(128)(4,1)}), s8[4194304]{0:T(1024)(128)(4,1)S(1)}, s32[]{:S(2)}) async-start(s8[4718592]{0:T(1024)(128)(4,1)} %bitcast.473), calls=%async_computation.10 | async-start | bytes 8388608
  260.8 33.7 %copy-start.8 = (f32[512,768]{1,0:T(8,128)}, f32[512,768]{1,0:T(8,128)S(1)}, u32[]{:S(2)}) copy-start(f32[512,768]{1,0:T(8,128)S(1)} %get-tuple-element.143) | copy-start | bytes 4718596
  261.2 19.8 %slice-start.11 = ((s8[4718592]{0:T(1024)(128)(4,1)}), s8[524288]{0:T(1024)(128)(4,1)S(1)}, s32[]{:S(2)}) async-start(s8[4718592]{0:T(1024)(128)(4,1)} %bitcast.473), calls=%async_computation.11 | async-start | bytes 1048576
  261.2 19.8 %copy-start.42 = (f32[768]{0:T(1024)S(1)}, f32[768]{0:T(1024)}, u32[]{:S(2)}) copy-start(f32[768]{0:T(1024)} %get-tuple-element.54) | copy-start | bytes 9220
  280.9 6.4 %slice-start.12 = ((s8[6291456]{0:T(1024)(128)(4,1)}), s8[4194304]{0:T(1024)(128)(4,1)S(1)}, s32[]{:S(2)}) async-start(s8[6291456]{0:T(1024)(128)(4,1)} %bitcast.519), calls=%async_computation.12 | async-start | bytes 8388608
  281.0 6.3 %slice-start.13 = ((s8[6291456]{0:T(1024)(128)(4,1)}), s8[2097152]{0:T(1024)(128)(4,1)S(1)}, s32[]{:S(2)}) async-start(s8[6291456]{0:T(1024)(128)(4,1)} %bitcast.519), calls=%async_computation.13 | async-start | bytes 4194304
  284.2 10.3 %slice-start.8 = ((s8[4718592]{0:T(1024)(128)(4,1)}), s8[4194304]{0:T(1024)(128)(4,1)S(1)}, s32[]{:S(2)}) async-start(s8[4718592]{0:T(1024)(128)(4,1)} %bitcast.470), calls=%async_computation.8 | async-start | bytes 8388608
  287.3 7.2 %copy-start.13 = (f32[512,768]{1,0:T(8,128)}, f32[512,768]{1,0:T(8,128)S(1)}, u32[]{:S(2)}) copy-start(f32[512,768]{1,0:T(8,128)S(1)} %get-tuple-element.75) | copy-start | bytes 4718596
  287.4 7.2 %slice-start.9 = ((s8[4718592]{0:T(1024)(128)(4,1)}), s8[524288]{0:T(1024)(128)(4,1)S(1)}, s32[]{:S(2)}) async-start(s8[4718592]{0:T(1024)(128)(4,1)} %bitcast.470), calls=%async_computation.9 | async-start | bytes 1048576
  302.1 11.3 %copy-start.10 = (f32[512,768]{1,0:T(8,128)}, f32[512,768]{1,0:T(8,128)S(1)}, u32[]{:S(2)}) copy-start(f32[512,768]{1,0:T(8,128)S(1)} %get-tuple-element.73) | copy-start | bytes 4718596
  302.1 6.0 copy-start.14
  302.1 6.2 copy-start.53
  320.3 7.8 %copy-start.18 = (bf16[2,384,512]{2,1,0:T(8,128)(2,1)}, bf16[2,384,512]{2,1,0:T(8,128)(2,1)S(1)}, u32[]{:S(2)}) copy-start(bf16[2,384,512]{2,1,0:T(8,128)(2,1)S(1)} %convolution_convert_fusion.9) | copy-start | bytes 2359300
  358.8 13.3 %copy-start.11 = (f32[512,768]{1,0:T(8,128)}, f32[512,768]{1,0:T(8,128)S(1)}, u32[]{:S(2)}) copy-start(f32[512,768]{1,0:T(8,128)S(1)} %get-tuple-element.71) | copy-start | bytes 4718596
  358.8 13.3 %slice-start.2 = ((s8[4718592]{0:T(1024)(128)(4,1)}), s8[4194304]{0:T(1024)(128)(4,1)S(1)}, s32[]{:S(2)}) async-start(s8[4718592]{0:T(1024)(128)(4,1)} %bitcast.456), calls=%async_computation.2 | async-start | bytes 8388608
  362.8 9.3 %copy-start.7 = (f32[512,768]{1,0:T(8,128)S(1)}, f32[512,768]{1,0:T(8,128)}, u32[]{:S(2)}) copy-start(f32[512,768]{1,0:T(8,128)} %copy-done.6) | copy-start | bytes 4718596
  362.8 9.3 %slice-start.3 = ((s8[4718592]{0:T(1024)(128)(4,1)}), s8[524288]{0:T(1024)(128)(4,1)S(1)}, s32[]{:S(2)}) async-start(s8[4718592]{0:T(1024)(128)(4,1)} %bitcast.456), calls=%async_computation.3 | async-start | bytes 1048576
  362.8 9.3 %copy-start.28 = (f32[512]{0:T(512)S(1)}, f32[512]{0:T(512)}, u32[]{:S(2)}) copy-start(f32[512]{0:T(512)} %copy-done.27) | copy-start | bytes 6148
  362.8 9.3 %copy-start.33 = (f32[768]{0:T(1024)S(1)}, f32[768]{0:T(1024)}, u32[]{:S(2)}) copy-start(f32[768]{0:T(1024)} %copy-done.32) | copy-start | bytes 9220
  362.8 9.3 %copy-start.38 = (f32[512]{0:T(512)S(1)}, f32[512]{0:T(512)}, u32[]{:S(2)}) copy-start(f32[512]{0:T(512)} %copy-done.37) | copy-start | bytes 6148
  372.1 5.3 copy-start.31
  372.1 5.3 copy-start.15
  384.2 6.5 %copy-start.12 = (f32[512,768]{1,0:T(8,128)S(1)}, f32[512,768]{1,0:T(8,128)}, u32[]{:S(2)}) copy-start(f32[512,768]{1,0:T(8,128)} %copy-done.11) | copy-start | bytes 4718596
  384.2 6.7 %copy-start.51 = (bf16[2,512,1536]{2,1,0:T(8,128)(2,1)S(1)}, bf16[2,512,1536]{2,1,0:T(8,128)(2,1)}, u32[]{:S(2)}) copy-start(bf16[2,512,1536]{2,1,0:T(8,128)(2,1)} %copy-done.50) | copy-start | bytes 9437188
  388.8 10.9 %copy-start.39 = (f32[512]{0:T(512)}, f32[512]{0:T(512)S(1)}, u32[]{:S(2)}) copy-start(f32[512]{0:T(512)S(1)} %negate_multiply_fusion.2) | copy-start | bytes 6148
  401.9 8.4 %copy-start.19 = (bf16[2,384,512]{2,1,0:T(8,128)(2,1)}, bf16[2,384,512]{2,1,0:T(8,128)(2,1)S(1)}, u32[]{:S(2)}) copy-start(bf16[2,384,512]{2,1,0:T(8,128)(2,1)S(1)} %convolution_convert_fusion.8) | copy-start | bytes 2359300
  401.9 12.1 %copy-start.16 = (bf16[2,512,384]{1,2,0:T(8,128)(2,1)S(1)}, bf16[2,512,384]{1,2,0:T(8,128)(2,1)}, u32[]{:S(2)}) copy-start(bf16[2,512,384]{1,2,0:T(8,128)(2,1)} %get-tuple-element.89) | copy-start | bytes 2359300
  414.0 7.3 %copy-start.25 = (f32[2,6,512]{2,1,0:T(8,128)S(1)}, f32[2,6,512]{2,1,0:T(8,128)}, u32[]{:S(2)}) copy-start(f32[2,6,512]{2,1,0:T(8,128)} %log_add_fusion) | copy-start | bytes 73732
  421.2 7.1 %copy-start.5 = (bf16[2,512,384]{1,2,0:T(8,128)(2,1)S(1)}, bf16[2,512,384]{1,2,0:T(8,128)(2,1)}, u32[]{:S(2)}) copy-start(bf16[2,512,384]{1,2,0:T(8,128)(2,1)} %copy-done.4) | copy-start | bytes 2359300
  441.1 5.8 copy-start.23
  441.1 5.8 copy-start.24
  441.2 5.8 copy-start.45
  (24 other events, 81.9 us)

commit v2 on v1

--- a/solution.py
+++ b/solution.py
@@ -10,7 +10,6 @@
 HEAD = 64
 EPS = 1e-06
 NEG = -1e30
-WAVES = 6
 NZ, NY, NC, NX = 4, 2, 2, 2
 MESH = pl.DeviceIdType.MESH
 BF = jnp.bfloat16
@@ -70,16 +69,50 @@
     dst[...] = now[...] + got[3] + got[4] + got[5]
 
 
-def gather_kernel(shard, small, full, small_out, got, acc, s_send, s_recv, own_sem, b_send, b_recv):
+def mm(a, b):
+    return jnp.dot(a, b, preferred_element_type=F32)
+
+
+def mm_nt(a, b):
+    return lax.dot_general(a, b, (((1,), (1,)), ((), ())), preferred_element_type=F32)
+
+
+def gelu_both(u):
+    bell = jnp.exp(u * u * -0.5)
+    t = 1.0 / (1.0 + (0.3275911 * 0.7071067811865476) * jnp.abs(u))
+    tail = 1.061405429 * 0.5 * t - 1.453152027 * 0.5
+    tail = tail * t + 1.421413741 * 0.5
+    tail = tail * t - 0.284496736 * 0.5
+    tail = (tail * t + 0.254829592 * 0.5) * t * bell
+    cdf = jnp.where(u < 0, tail, 1.0 - tail)
+    return u * cdf, cdf + u * bell * 0.3989422804014327
+
+
+def norm_parts(r):
+    average = jnp.mean(r, axis=-1, keepdims=True)
+    centred = r - average
+    variance = jnp.mean(centred * centred, axis=-1, keepdims=True)
+    rstd = lax.rsqrt(variance + EPS)
+    return centred * rstd, rstd
+
+
+def block(i, n):
+    return pl.ds(pl.multiple_of(i * n, n), n)
+
+
+FWAVES = 12
+AHEAD = 2
+SIDE = FWAVES - 1
+
+
+def gather_steps(shard, full, own_sem, sems, side_sems):
     z, y, c, t = place()
     core, over_x, over_y, over_z = partners()
-    greet([core, over_x, over_y] + over_z)
     half = shard.shape[2] // 2
     lo, hi = pl.ds(0, half), pl.ds(half, half)
-    sems = (b_send, b_recv)
     owns, first, second, third, last = {}, {}, {}, {}, {}
 
-    def start_first(k):
+    def one(k):
         owns[k] = pltpu.make_async_copy(shard.at[k], full.at[k, t, z, y, c], own_sem.at[k])
         owns[k].start()
         first[k] = [
@@ -87,7 +120,7 @@
             for j, other in enumerate(over_z)
         ]
 
-    def start_second(k):
+    def two(k):
         owns[k].wait()
         for copy in first[k]:
             copy.wait()
@@ -95,49 +128,411 @@
         b = full.at[k, t, :, y, c, :, hi]
         second[k] = [send(a, a, sems, (k, 3), over_y), send(b, b, sems, (k, 4), over_x)]
 
-    def start_third(k):
+    def three(k):
         for copy in second[k]:
             copy.wait()
         a = full.at[k, t, :, :, c, :, lo]
         b = full.at[k, :, :, y, c, :, hi]
         third[k] = [send(a, a, sems, (k, 5), over_x), send(b, b, sems, (k, 6), over_y)]
 
-    def start_last(k):
+    def four(k):
         for copy in third[k]:
             copy.wait()
         a = full.at[k, :, :, :, c]
         last[k] = send(a, a, sems, (k, 7), core)
 
-    start_first(0)
-    start_first(1)
-    small_sum(small, small_out, got, acc, (s_send, s_recv))
-    for step in range(WAVES + 2):
-        if step < WAVES:
-            start_second(step)
-            if step + 2 < WAVES:
-                start_first(step + 2)
-        if 0 <= step - 1 < WAVES:
-            start_third(step - 1)
-        if 0 <= step - 2 < WAVES:
-            start_last(step - 2)
-    for k in range(WAVES):
+    def five(k):
         last[k].wait()
 
-
-def gather_all(shard, small):
-    waves, rows, cols = shard.shape
+    side = {}
+
+    def side_one():
+        owns[SIDE] = pltpu.make_async_copy(shard.at[SIDE], full.at[SIDE, t, z, y, c], own_sem.at[SIDE])
+        owns[SIDE].start()
+        mine = full.at[SIDE, t, z, y, c]
+        side[1] = [
+            send(shard.at[SIDE, :, lo], mine.at[:, lo], side_sems, 0, over_x),
+            send(shard.at[SIDE, :, hi], mine.at[:, hi], side_sems, 1, over_y),
+        ]
+
+    def side_two():
+        owns[SIDE].wait()
+        for copy in side[1]:
+            copy.wait()
+        a = full.at[SIDE, :, z, y, c, :, lo]
+        b = full.at[SIDE, t, z, :, c, :, hi]
+        side[2] = [send(a, a, side_sems, 2, over_y), send(b, b, side_sems, 3, over_x)]
+
+    def side_three(i):
+        if i == 0:
+            for copy in side[2]:
+                copy.wait()
+            side[3] = []
+        a = full.at[SIDE, i // 2, z, i % 2, c]
+        side[3] += [send(a, a, side_sems, 4 + 3 * i + j, other) for j, other in enumerate(over_z)]
+
+    def side_four():
+        for copy in side[3]:
+            copy.wait()
+        a = full.at[SIDE, :, :, :, c]
+        last[SIDE] = send(a, a, sems, (SIDE, 7), core)
+
+    return one, two, three, four, five, (side_one, side_two, side_three, side_four)
+
+
+def sum_steps(src, dst, got, acc, sems):
+    core, over_x, over_y, over_z = partners()
+    flying = {}
+
+    def begin():
+        flying[0] = [send(src, got.at[0], sems, 0, core)]
+
+    def middle(step, other):
+        for copy in flying[step - 1]:
+            copy.wait()
+        before = src if step == 1 else acc.at[step - 2]
+        acc[step - 1] = before[...] + got[step - 1]
+        if step < 3:
+            flying[step] = [send(acc.at[step - 1], got.at[step], sems, step, other)]
+        else:
+            flying[step] = [send(acc.at[2], got.at[3 + j], sems, 3 + j, o) for j, o in enumerate(over_z)]
+
+    def end():
+        for copy in flying[3]:
+            copy.wait()
+        dst[...] = acc[2] + got[3] + got[4] + got[5]
+
+    return [begin, lambda: middle(1, over_x), lambda: middle(2, over_y), lambda: middle(3, None), end]
+
+
+SAVED = ("x", "q", "k", "v", "probs", "o", "z1", "rstd1", "h", "g", "gp", "z2", "rstd2")
+
+
+def pack_copies(raw, shard, r_bias, r_up, r_norm, sem):
+    pieces = {"small": []}
+    width = shard.shape[2]
+    half = width // 2
+    count = 0
+
+    def copy(src, dst):
+        nonlocal count
+        count += 1
+        return pltpu.make_async_copy(src, dst, sem.at[count - 1])
+
+    for layer in range(2):
+        wq, bq, wk, wv, bv, wo, bo, g1, s1, wu, bu, wd, bd, g2, s2 = raw[layer]
+        at = 6 * layer
+        pieces[f"qk{layer}"] = [copy(wq, shard.at[at, :, :half]), copy(wk, shard.at[at, :, half:])]
+        pieces[f"vo{layer}"] = [copy(wv, shard.at[at + 1, :, :half]), copy(wo, shard.at[at + 1, :, half:])]
+        pieces[f"u{layer}"] = [
+            copy(wu.at[:, :width], shard.at[at + 2]),
+            copy(wu.at[:, width:], shard.at[at + 3]),
+        ]
+        pieces[f"d{layer}"] = [
+            copy(wd.at[:, :width], shard.at[at + 4]),
+            copy(wd.at[:, width:], shard.at[at + 5]),
+        ]
+        pieces["small"] += [copy(bq, r_bias.at[2 * layer]), copy(bv, r_bias.at[2 * layer + 1])]
+        pieces["small"] += [copy(bu, r_up.at[layer])]
+        pieces["small"] += [copy(v, r_norm.at[6 * layer + i]) for i, v in enumerate((bo, g1, s1, bd, g2, s2))]
+    return pieces
+
+
+def one_hot(rows, columns, start, axis):
+    a = lax.broadcasted_iota(jnp.int32, (rows, columns), axis)
+    b = lax.broadcasted_iota(jnp.int32, (rows, columns), 1 - axis)
+    return jnp.where(a == b + start, 1.0, 0.0).astype(F32)
+
+
+def mm_exact(a, b):
+    return jnp.dot(a, b, preferred_element_type=F32, precision=lax.Precision.HIGHEST)
+
+
+def spread_small(small, r_bias, r_up, r_norm, dp, t, n_dp):
+    width = small.shape[1]
+    m = r_norm.shape[2]
+    to_norm = one_hot(m, width, (2 * dp + t) * m, 1)
+    to_bias = one_hot(m, width, (t * n_dp + dp) * m, 1)
+    many = r_up.shape[2]
+    biases = mm_exact(jnp.concatenate([r_bias[i].astype(F32) for i in range(4)], axis=0), to_bias)
+    norms = mm_exact(jnp.concatenate([r_norm[i] for i in range(12)], axis=0), to_norm)
+    ups = jnp.concatenate([r_up[i].astype(F32) for i in range(2)], axis=0)
+    for layer in range(2):
+        at = 12 * layer
+        small[at : at + 2, :] = biases[2 * layer : 2 * layer + 2]
+        small[at + 2 : at + 8, :] = norms[6 * layer : 6 * layer + 6]
+    for i in range(4):
+        r = mm_exact(ups, one_hot(many, width, (t * n_dp + dp) * many - i * width, 1))
+        for layer in range(2):
+            small[12 * layer + 8 + i : 12 * layer + 9 + i, :] = r[layer : layer + 1]
+
+
+def forward_kernel(*refs):
+    lengths, rows = refs[:2]
+    raw = [refs[2 + 15 * i : 17 + 15 * i] for i in range(2)]
+    refs = refs[32:]
+    full, small_out, act_out = refs[:3]
+    saves = [dict(zip(SAVED, refs[3 + 13 * i : 16 + 13 * i])) for i in range(2)]
+    refs = refs[29:]
+    shard, small, r_bias, r_up, r_norm, raw_sem, x_sem = refs[:7]
+    refs = refs[7:]
+    bufs = dict(zip(SAVED, refs[:13]))
+    bias, vt, ot, r2, w_slots, got, acc, s_send, s_recv, own_sem, b_send, b_recv, c_send, c_recv, load_sem, save_sem = refs[13:]
+    z, y, c, t_mine = place()
+    dp = lax.axis_index("dp")
+    core, over_x, over_y, over_z = partners()
+    pieces = pack_copies(raw, shard, r_bias, r_up, r_norm, raw_sem)
+    x_copy = pltpu.make_async_copy(rows, bufs["x"], x_sem)
+    for name in ("qk0", "d1", "small", "vo0", "u0", "d0", "qk1", "vo1", "u1"):
+        for copy in pieces[name]:
+            copy.start()
+        if name == "vo0":
+            x_copy.start()
+    greet([core, over_x, over_y] + over_z)
+    one, two, three, four, five, side = gather_steps(
+        shard, full, own_sem, (b_send, b_recv), (c_send, c_recv)
+    )
+    sums = sum_steps(small, small_out, got, acc, (s_send, s_recv))
+    loads, stores = {}, {}
+    n, width = rows.shape
+    half = width // 2
+
+    def packed(name):
+        for copy in pieces[name]:
+            copy.wait()
+
+    packed("qk0")
+    one(0)
+    packed("d1")
+    side[0]()
+    packed("small")
+    n_dp = lax.axis_size("dp")
+    spread_small(small, r_bias, r_up, r_norm, dp, t_mine, n_dp)
+    sums[0]()
+    side[1]()
+    packed("vo0")
+    one(1)
+    x_copy.wait()
+    for name in ("u0", "d0", "qk1", "vo1", "u1"):
+        packed(name)
+    length = lengths[t_mine]
+    inside = lax.broadcasted_iota(jnp.int32, (n, 1), 0) < length
+    bias[...] = jnp.where(inside, 0.0, NEG)
+
+    def bring(k):
+        five(k)
+        loads[k] = pltpu.make_async_copy(full.at[k], w_slots.at[k % 2], load_sem.at[k % 2])
+        loads[k].start()
+
+    def comm(step):
+        if step + 1 < len(sums):
+            sums[step + 1]()
+        if step < SIDE:
+            two(step)
+            if step + AHEAD < SIDE:
+                one(step + AHEAD)
+        if step % 2 == 1 and step < 8:
+            side[2](step // 2)
+        if 0 <= step - 1 < SIDE:
+            three(step - 1)
+        if step == SIDE - 1:
+            side[3]()
+        if 0 <= step - 2 < SIDE:
+            four(step - 2)
+        if 0 <= step - 3 < FWAVES:
+            bring(step - 3)
+
+    def weights(k):
+        loads[k].wait()
+        slot = w_slots.at[k % 2]
+        return lambda t, lanes: slot[t, :, :, :, :, lanes].reshape(width, -1)
+
+    def save(layer, *names):
+        for name in names:
+            copy = pltpu.make_async_copy(bufs[name], saves[layer][name], save_sem.at[SAVED.index(name)])
+            copy.start()
+            stores[name] = copy
+
+    def free(*names):
+        for name in names:
+            if name in stores:
+                stores.pop(name).wait()
+
+    def vec(layer, i):
+        return small_out[12 * layer + i : 12 * layer + i + 1]
+
+    def scores_stage(layer, k):
+        w = weights(k)
+        x, q, kk, probs = (bufs[i] for i in ("x", "q", "k", "probs"))
+        free("q", "k", "probs")
+        for t in range(2):
+            here = slice(t * half, (t + 1) * half)
+            r = mm(x[...], w(t, slice(0, half))) + vec(layer, 0)[:, here]
+            q[:, here] = r.astype(BF) * BF(HEAD**-0.5)
+            kk[:, here] = mm(x[...], w(t, slice(half, width))).astype(BF)
+        save(layer, "q", "k")
+        lane = lax.broadcasted_iota(jnp.int32, (1, 128), 1)
+
+        @pl.loop(0, width // 128)
+        def _(p):
+            kp = kk[:, block(p, 128)]
+            qp = q[:, block(p, 128)]
+            for head in range(2):
+                qm = jnp.where((lane >= HEAD) == (head == 1), qp, BF(0))
+                s = mm_nt(kp, qm) + bias[...]
+                e = jnp.exp(s - jnp.max(s, axis=0, keepdims=True))
+                probs[2 * p + head] = (e * (1.0 / jnp.sum(e, axis=0, keepdims=True))).astype(BF)
+
+        save(layer, "probs")
+
+    def attend_stage(layer, k):
+        w = weights(k)
+        x, v, probs, o, z1, rstd1, h = (bufs[i] for i in ("x", "v", "probs", "o", "z1", "rstd1", "h"))
+        free("v", "o", "z1", "rstd1", "h")
+        for t in range(2):
+            here = slice(t * half, (t + 1) * half)
+            r = mm(x[...], w(t, slice(0, half))) + vec(layer, 1)[:, here]
+            v[:, here] = r.astype(BF)
+        save(layer, "v")
+        vt[...] = v[...].T
+
+        @pl.loop(0, width // HEAD)
+        def _(i):
+            ot[block(i, HEAD), :] = mm(vt[block(i, HEAD), :], probs[i]).astype(BF)
+
+        o[...] = ot[...].T
+        save(layer, "o")
+        r = x[...].astype(F32) + vec(layer, 2)
+        for t in range(2):
+            r = r + mm_nt(o[:, t * half : (t + 1) * half], w(t, slice(half, width)))
+        z, rstd = norm_parts(r)
+        z1[...] = z.astype(BF)
+        rstd1[...] = rstd
+        h[...] = (z * vec(layer, 3) + vec(layer, 4)).astype(BF)
+        save(layer, "x", "z1", "rstd1", "h")
+
+    def up_stage(layer, k, part):
+        w = weights(k)
+        h, g, gp = (bufs[i] for i in ("h", "g", "gp"))
+        if part == 0:
+            free("g", "gp")
+        step = 384
+        for t in range(2):
+
+            @pl.loop(0, width // step)
+            def _(i):
+                at = t * 2 * width + part * width + i * step
+                here = pl.ds(pl.multiple_of(part * width + i * step, step), step)
+                u = mm(h[...], w(t, block(i, step)))
+                bu = bu_row(layer, t, part, i, step)
+                a, b = gelu_both(u + bu)
+                g[t, :, here] = a.astype(BF)
+                gp[t, :, here] = b.astype(BF)
+
+        if part == 1:
+            save(layer, "g", "gp")
+
+    def bu_row(layer, t, part, i, step):
+        return small_out[pl.ds(12 * layer + 8 + 2 * t + part, 1), block(i, step)]
+
+    def down_stage(layer, k, part):
+        w = weights(k)
+        h, g, z2, rstd2 = (bufs[i] for i in ("h", "g", "z2", "rstd2"))
+        here = slice(part * width, (part + 1) * width)
+        total = None
+        for t in range(2):
+            r = mm_nt(g[t, :, here], w(t, slice(0, width)))
+            total = r if total is None else total + r
+        if part == 0:
+            r2[...] = total
+            return
+        free("z2", "rstd2", "x")
+        r = r2[...] + total + h[...].astype(F32) + vec(layer, 5)
+        z, rstd = norm_parts(r)
+        z2[...] = z.astype(BF)
+        rstd2[...] = rstd
+        result = z * vec(layer, 6) + vec(layer, 7)
+        save(layer, "z2", "rstd2")
+        if layer == 0:
+            bufs["x"][...] = result.astype(BF)
+        else:
+            act_out[...] = jnp.where(inside, result, 0.0).astype(BF)
+
+    def compute(k):
+        layer, i = k // 6, k % 6
+        if i == 0:
+            scores_stage(layer, k)
+        elif i == 1:
+            attend_stage(layer, k)
+        elif i < 4:
+            up_stage(layer, k, i - 2)
+        else:
+            down_stage(layer, k, i - 4)
+
+    for step in range(FWAVES + 4):
+        comm(step)
+        if step >= 4:
+            compute(step - 4)
+    free(*list(stores))
+
+
+def saved_kinds(n, width):
+    heads = width // HEAD
+    return {
+        "x": ((n, width), BF),
+        "q": ((n, width), BF),
+        "k": ((n, width), BF),
+        "v": ((n, width), BF),
+        "probs": ((heads, n, n), BF),
+        "o": ((n, width), BF),
+        "z1": ((n, width), BF),
+        "rstd1": ((n, 1), F32),
+        "h": ((n, width), BF),
+        "g": ((2, n, 2 * width), BF),
+        "gp": ((2, n, 2 * width), BF),
+        "z2": ((n, width), BF),
+        "rstd2": ((n, 1), F32),
+    }
+
+
+def forward_all(lengths, rows, teacher, student):
+    n, width = rows.shape
+    part = teacher[0].shape[0]
+    waves, cols = FWAVES, width
+    raw = teacher + student
+    few, many = raw[1].shape[1], raw[10].shape[1]
+    small = jax.ShapeDtypeStruct((24, width), F32)
+    kinds = saved_kinds(n, width)
     dma = pltpu.SemaphoreType.DMA
-    any_spec = pl.BlockSpec(memory_space=pl.ANY)
+    hbm = pl.BlockSpec(memory_space=pltpu.MemorySpace.HBM)
     vmem = pl.BlockSpec(memory_space=pltpu.VMEM)
-    full, small_out = pl.pallas_call(
-        gather_kernel,
+    shape = jax.ShapeDtypeStruct
+    outs = pl.pallas_call(
+        forward_kernel,
         out_shape=(
-            jax.ShapeDtypeStruct((waves, NX, NZ, NY, NC, rows, cols), BF),
-            jax.ShapeDtypeStruct(small.shape, F32),
-        ),
-        in_specs=[any_spec, vmem],
-        out_specs=(any_spec, vmem),
+            shape((waves, NX, NZ, NY, NC, part, cols), BF),
+            shape(small.shape, F32),
+            shape((n, width), BF),
+        )
+        + tuple(shape(*kinds[name]) for name in SAVED) * 2,
+        in_specs=[pl.BlockSpec(memory_space=pltpu.SMEM)] + [hbm] * 31,
+        out_specs=(hbm, vmem, vmem) + (hbm,) * 26,
         scratch_shapes=[
+            pltpu.VMEM((waves, part, cols), BF),
+            pltpu.VMEM(small.shape, F32),
+            pltpu.VMEM((4, 1, few), BF),
+            pltpu.VMEM((2, 1, many), BF),
+            pltpu.VMEM((12, 1, few), F32),
+            dma((34,)),
+            dma(()),
+        ]
+        + [pltpu.VMEM(*kinds[name]) for name in SAVED]
+        + [
+            pltpu.VMEM((n, 1), F32),
+            pltpu.VMEM((width, n), BF),
+            pltpu.VMEM((width, n), BF),
+            pltpu.VMEM((n, width), F32),
+            pltpu.VMEM((2, NX, NZ, NY, NC, part, cols), BF),
             pltpu.VMEM((6,) + small.shape, F32),
             pltpu.VMEM((3,) + small.shape, F32),
             dma((6,)),
@@ -145,134 +540,585 @@
             dma((waves,)),
             dma((waves, 8)),
             dma((waves, 8)),
+            dma((16,)),
+            dma((16,)),
+            dma((2,)),
+            dma((13,)),
         ],
-        name="gather_all",
+        name="forward_all",
         compiler_params=pltpu.CompilerParams(
-            collective_id=0, has_side_effects=True, vmem_limit_bytes=32 << 20
+            collective_id=0, has_side_effects=True, vmem_limit_bytes=60 << 20
         ),
-    )(shard, small)
-    return full.reshape(waves, NX, NZ * NY * NC * rows, cols), small_out
-
-
-def reduce_kernel(*refs):
-    parts, refs = refs[:WAVES], refs[WAVES:]
-    small, out, small_out, own, rc, r2a, r2b, r3a, r3b, r4, got, acc, s_send, s_recv, own_sem, b_send, b_recv = refs
+    )(lengths, rows, *raw)
+    full, small, activations = outs[:3]
+    saved = [dict(zip(SAVED, outs[3 + 13 * i : 16 + 13 * i])) for i in range(2)]
+    return full, small, activations, saved
+
+
+ORDER = [6 + i for i in (4, 5, 2, 3, 1, 0)] + [4, 5, 2, 3, 1, 0]
+RC, R2S, R3S = 7, 3, 3
+TURN = 1
+RESTS = 16
+WAITS = (1, 5, 4, 8)
+LAST = FWAVES - 1
+CUTS = 3
+
+
+def reduce_steps(stage, rc, r2a, r2b, r3a, r3b, r4, rz, ra, rb, out, credit, sems, t_sems):
     z, y, c, t = place()
     core, over_x, over_y, over_z = partners()
-    greet([core, over_x, over_y] + over_z)
     half = out.shape[2] // 2
     lo, hi = pl.ds(0, half), pl.ds(half, half)
-    sems = (b_send, b_recv)
-    local, first, second, third, last = {}, {}, {}, {}, {}
-
-    def start_first(k):
-        local[k] = pltpu.make_async_copy(parts[k].at[:, :, :, c], own.at[k % 2], own_sem.at[k % 2])
-        local[k].start()
-        first[k] = send(parts[k].at[:, :, :, 1 - c], rc.at[k], sems, (k, 0), core)
-
-    def start_second(k):
-        local[k].wait()
-        first[k].wait()
-
+    flying = {}
+
+    def rest():
+        pass
+
+    def wait(key):
+        for copy in flying.pop(key):
+            copy.wait()
+
+    def give(kind, other):
+        pl.semaphore_signal(credit.at[kind], inc=1, device_id=other, device_id_type=MESH)
+
+    def add(dst, *srcs):
+        total = dst[...]
+        for src in srcs:
+            total = total + src[...]
+        dst[...] = total
+
+    def own(s, j, lanes):
         @pl.loop(0, NZ)
         def _(i):
             for a in range(NX):
                 for b in range(NY):
-                    rc[k, a, i, b] = rc[k, a, i, b] + own[k % 2, a, i, b]
-
-        second[k] = [
-            send(rc.at[k, 1 - t, :, :, :, lo], r2a.at[k], sems, (k, 1), over_x),
-            send(rc.at[k, :, :, 1 - y, :, hi], r2b.at[k], sems, (k, 2), over_y),
-        ]
-
-    def start_third(k):
-        for copy in second[k]:
-            copy.wait()
-
-        @pl.loop(0, NZ)
-        def _(i):
+                    for lane in lanes:
+                        add(rc.at[s, a, i, b, :, lane], stage.at[j % 2, a, i, b, c, :, lane])
+
+    def steps(j, cut=None):
+        n = j if TURN < 0 or j < TURN else j - 1
+        total = FWAVES - (TURN >= 0)
+        key, s, s2, s3 = (j, cut), n % RC, n % R2S, n % R3S
+        row = j if cut is None else FWAVES + cut
+        first = cut in (None, 0)
+        width = half if cut is None else half // CUTS
+        at = 0 if cut is None else cut * width
+        low, high = pl.ds(at, width), pl.ds(half + at, width)
+        spans = [pl.ds(0, 2 * half)] if cut is None else [low, high]
+
+        def one():
+            if n >= RC and first:
+                pl.semaphore_wait(credit.at[0], 1)
+            flying[key] = [
+                send(stage.at[j % 2, :, :, :, 1 - c, :, lanes], rc.at[s, :, :, :, :, lanes], sems, (row, i), core)
+                for i, lanes in enumerate(spans)
+            ]
+
+        def two():
+            wait(key)
+            own(s, j, spans)
+            if n >= R2S and first:
+                pl.semaphore_wait(credit.at[1], 1)
+                pl.semaphore_wait(credit.at[2], 1)
+            flying[key] = [
+                send(rc.at[s, 1 - t, :, :, :, low], r2a.at[s2, :, :, :, low], sems, (row, 2), over_x),
+                send(rc.at[s, :, :, 1 - y, :, high], r2b.at[s2, :, :, :, low], sems, (row, 3), over_y),
+            ]
+
+        def three():
+            wait(key)
+
+            @pl.loop(0, NZ)
+            def _(i):
+                for b in range(2):
+                    add(rc.at[s, t, i, b, :, low], r2a.at[s2, i, b, :, low])
+                    add(rc.at[s, b, i, y, :, high], r2b.at[s2, b, i, :, low])
+
+            if n + R2S < total:
+                give(1, over_x)
+                give(2, over_y)
+            if n >= R3S and first:
+                pl.semaphore_wait(credit.at[3], 1)
+                pl.semaphore_wait(credit.at[4], 1)
+            flying[key] = [
+                send(rc.at[s, t, :, 1 - y, :, low], r3a.at[s3, :, :, low], sems, (row, 4), over_y),
+                send(rc.at[s, 1 - t, :, y, :, high], r3b.at[s3, :, :, low], sems, (row, 5), over_x),
+            ]
+
+        def four():
+            wait(key)
+
+            @pl.loop(0, NZ)
+            def _(i):
+                add(rc.at[s, t, i, y, :, low], r3a.at[s3, i, :, low])
+                add(rc.at[s, t, i, y, :, high], r3b.at[s3, i, :, low])
+
+            if n + R3S < total:
+                give(3, over_y)
+                give(4, over_x)
+            flying[key] = [
+                send(
+                    rc.at[s, t, lax.rem(z + i + 1, NZ), y, :, lanes],
+                    r4.at[n, i, :, lanes],
+                    sems,
+                    (row, 6 + 3 * k + i),
+                    other,
+                )
+                for i, other in enumerate(over_z)
+                for k, lanes in enumerate(spans)
+            ]
+
+        def five():
+            wait(key)
+            for lanes in spans:
+                value = rc[s, t, z, y, :, lanes].astype(F32)
+                for i in range(3):
+                    value = value + r4[n, i, :, lanes].astype(F32)
+                out[ORDER[j], :, lanes] = value
+            if n + RC < total:
+                give(0, core)
+
+        return [one] + [rest] * WAITS[0] + [two] + [rest] * WAITS[1] + [three] + [rest] * WAITS[2] + [four] + [rest] * WAITS[3] + [five]
+
+    def turned(j):
+        s = RC
+
+        def one():
+            flying[j] = [send(stage.at[j % 2, :, :, :, 1 - c], rc.at[s], t_sems, 0, core)]
+
+        def two():
+            wait(j)
+            own(s, j, [pl.ds(0, 2 * half)])
+            flying[j] = [
+                send(rc.at[s, :, lax.rem(z + i + 1, NZ)], rz.at[i], t_sems, 1 + i, other)
+                for i, other in enumerate(over_z)
+            ]
+
+        def three():
+            wait(j)
+            for a in range(NX):
+                for b in range(NY):
+                    add(rc.at[s, a, z, b], rz.at[0, a, b], rz.at[1, a, b], rz.at[2, a, b])
+            flying[j] = [
+                send(rc.at[s, 1 - t, z, :, :, lo], ra.at[0:2], t_sems, 4, over_x),
+                send(rc.at[s, :, z, 1 - y, :, hi], rb.at[0:2], t_sems, 5, over_y),
+            ]
+
+        def four():
+            wait(j)
             for b in range(2):
-                rc[k, t, i, b, :, lo] = rc[k, t, i, b, :, lo] + r2a[k, i, b]
-                rc[k, b, i, y, :, hi] = rc[k, b, i, y, :, hi] + r2b[k, b, i]
-
-        third[k] = [
-            send(rc.at[k, t, :, 1 - y, :, lo], r3a.at[k], sems, (k, 3), over_y),
-            send(rc.at[k, 1 - t, :, y, :, hi], r3b.at[k], sems, (k, 4), over_x),
-        ]
-
-    def start_last(k):
-        for copy in third[k]:
-            copy.wait()
-
-        @pl.loop(0, NZ)
-        def _(i):
-            rc[k, t, i, y, :, lo] = rc[k, t, i, y, :, lo] + r3a[k, i]
-            rc[k, t, i, y, :, hi] = rc[k, t, i, y, :, hi] + r3b[k, i]
-
-        last[k] = [
-            send(rc.at[k, t, lax.rem(z + j + 1, NZ), y], r4.at[k, j], sems, (k, 5 + j), other)
-            for j, other in enumerate(over_z)
-        ]
-
-    def finish(k):
-        for copy in last[k]:
-            copy.wait()
-        total = rc[k, t, z, y].astype(F32)
-        for j in range(3):
-            total = total + r4[k, j].astype(F32)
-        out[k] = total
-
-    start_first(0)
-    for step in range(WAVES + 3):
-        if step < WAVES:
-            if step + 1 < WAVES:
-                start_first(step + 1)
-            start_second(step)
-        if 0 <= step - 1 < WAVES:
-            start_third(step - 1)
-        if 0 <= step - 2 < WAVES:
-            start_last(step - 2)
-        if 0 <= step - 3 < WAVES:
-            finish(step - 3)
-    small_sum(small, small_out, got, acc, (s_send, s_recv))
-
-
-def reduce_all(parts, small):
-    _, width, cols = parts[0].shape
-    rows = width // (NZ * NY * NC)
-    shaped = [part.reshape(NX, NZ, NY, NC, rows, cols) for part in parts]
+                add(rc.at[s, t, z, b, :, lo], ra.at[b])
+                add(rc.at[s, b, z, y, :, hi], rb.at[b])
+            flying[j] = [
+                send(rc.at[s, t, z, 1 - y, :, lo], ra.at[2], t_sems, 6, over_y),
+                send(rc.at[s, 1 - t, z, y, :, hi], rb.at[2], t_sems, 7, over_x),
+            ]
+
+        def five():
+            wait(j)
+            out[ORDER[j], :, lo] = rc[s, t, z, y, :, lo].astype(F32) + ra[2].astype(F32)
+            out[ORDER[j], :, hi] = rc[s, t, z, y, :, hi].astype(F32) + rb[2].astype(F32)
+
+        return [one, two] + [rest] * RESTS + [three, rest, rest, four, rest, rest, five]
+
+    return steps, turned
+
+
+def back_kernel(*refs):
+    lengths, grad, small, full = refs[:4]
+    saves = [dict(zip(SAVED, refs[4 + 13 * i : 17 + 13 * i])) for i in range(2)]
+    refs = refs[30:]
+    d_input, out, small_out = refs[:3]
+    refs = refs[3:]
+    bufs = dict(zip(SAVED, refs[:13]))
+    refs = refs[13:]
+    dy, dr, dlo, lot, dlot, d_o, dq, dk, dv, kt, dqt = refs[:11]
+    refs = refs[11:]
+    w_slots, stage, rc, r2a, r2b, r3a, r3b, r4, rz, ra, rb, terms, got, acc = refs[:14]
+    s_send, s_recv, b_send, b_recv, t_send, t_recv, credit, load_sem, w_sem = refs[14:]
+    core, over_x, over_y, over_z = partners()
+    n, width = grad.shape
+    half = width // 2
+    loads, w_loads = {}, {}
+
+    def load(layer, *names):
+        for name in names:
+            copy = pltpu.make_async_copy(saves[layer][name], bufs[name], load_sem.at[SAVED.index(name)])
+            copy.start()
+            loads[name] = copy
+
+    def need(*names):
+        for name in names:
+            if name in loads:
+                loads.pop(name).wait()
+
+    def fetch(j):
+        if j < FWAVES:
+            w_loads[j] = pltpu.make_async_copy(full.at[ORDER[j]], w_slots.at[j % 2], w_sem.at[j % 2])
+            w_loads[j].start()
+
+    def weights(j):
+        w_loads[j].wait()
+        slot = w_slots.at[j % 2]
+        return lambda t, lanes: slot[t, :, :, :, :, lanes].reshape(width, -1)
+
+    load(1, "z2", "rstd2")
+    fetch(0)
+    load(1, "g", "gp", "h", "z1", "rstd1")
+    fetch(1)
+    load(1, "o", "probs", "x", "v", "k", "q")
+    greet([core, over_x, over_y] + over_z)
+    steps, turned = reduce_steps(
+        stage, rc, r2a, r2b, r3a, r3b, r4, rz, ra, rb, out, credit, (b_send, b_recv), (t_send, t_recv)
+    )
+    moving = []
+
+    def advance():
+        for item in moving:
+            item.pop(0)()
+        moving[:] = [item for item in moving if item]
+
+    def comm(j, cut=None):
+        advance()
+        item = turned(j) if j == TURN else steps(j, cut)
+        item.pop(0)()
+        moving.append(item)
+
+    def put(j, t, lanes, value):
+        stage[j % 2, t, :, :, :, :, lanes] = value.astype(BF).reshape(NZ, NY, NC, -1, value.shape[1])
+
+    def term(layer, i, value):
+        terms[12 * layer + i : 12 * layer + i + 1, :] = value
+
+    def vec(layer, i):
+        return small[12 * layer + i : 12 * layer + i + 1]
+
+    def norm_back(layer, at, d_out, z, rstd):
+        zf = z[...].astype(F32)
+        dz = d_out * vec(layer, at + 1)
+        a = jnp.mean(dz, axis=-1, keepdims=True)
+        b = jnp.mean(dz * zf, axis=-1, keepdims=True)
+        d_in = rstd[...] * (dz - a - zf * b)
+        term(layer, at, jnp.sum(d_in, axis=0, keepdims=True))
+        term(layer, at + 1, jnp.sum(d_out * zf, axis=0, keepdims=True))
+        term(layer, at + 2, jnp.sum(d_out, axis=0, keepdims=True))
+        dr[...] = d_in
+        low = d_in.astype(BF)
+        dlo[...] = low
+        dlot[...] = low.T
+
+    def down_stage(layer, j, part):
+        g, gp = bufs["g"], bufs["gp"]
+        if part == 0:
+            need("z2", "rstd2")
+            norm_back(layer, 5, dy[...], bufs["z2"], bufs["rstd2"])
+            need("g", "gp")
+        w = weights(j)
+        here = slice(part * width, (part + 1) * width)
+        for t in range(2):
+            put(j, t, slice(0, width), mm(dlot[...], g[t, :, here]))
+            if t == 0:
+                advance()
+        comm(j)
+        for t in range(2):
+            if t == 1:
+                advance()
+            du = (mm(dlo[...], w(t, slice(0, width))) * gp[t, :, here].astype(F32)).astype(BF)
+            gp[t, :, here] = du
+            term(layer, 8 + 2 * t + part, jnp.sum(du.astype(F32), axis=0, keepdims=True))
+        fetch(j + 2)
+        if part == 1 and layer == 1:
+            load(0, "z2", "rstd2", "g")
+
+    def up_stage(layer, j, part):
+        h, gp = bufs["h"], bufs["gp"]
+        if part == 0:
+            need("h")
+            lot[...] = h[...].T
+        w = weights(j)
+        here = slice(part * width, (part + 1) * width)
+        for t in range(2):
+            put(j, t, slice(0, width), mm(lot[...], gp[t, :, here]))
+            if t == 0:
+                advance()
+        comm(j)
+        for t in range(2):
+            if t == 1:
+                advance()
+            dr[...] = dr[...] + mm_nt(gp[t, :, here], w(t, slice(0, width)))
+        fetch(j + 2)
+        if part == 0:
+            return
+        total = dr[...]
+        need("z1", "rstd1")
+        norm_back(layer, 2, total, bufs["z1"], bufs["rstd1"])
+        if layer == 1:
+            load(0, "gp", "h", "z1", "rstd1")
+
+    lane = lax.broadcasted_iota(jnp.int32, (1, 128), 1)
+
+    def of_head(head, value):
+        return jnp.where((lane >= HEAD) == (head == 1), value, BF(0))
+
+    def value_stage(layer, j):
+        o, probs, x = bufs["o"], bufs["probs"], bufs["x"]
+        w = weights(j)
+        need("o", "probs", "x")
+        for t in range(2):
+            here = slice(t * half, (t + 1) * half)
+            put(j, t, slice(half, width), mm(dlot[...], o[:, here]))
+            d_o[:, here] = mm(dlo[...], w(t, slice(half, width))).astype(BF)
+        lot[...] = x[...].T
+        advance()
+
+        @pl.loop(0, width // 128)
+        def _(p):
+            dop = d_o[:, block(p, 128)]
+            total = mm(probs[2 * p], of_head(0, dop)) + mm(probs[2 * p + 1], of_head(1, dop))
+            dv[:, block(p, 128)] = total.astype(BF)
+
+        advance()
+        for t in range(2):
+            put(j, t, slice(0, half), mm(lot[...], dv[:, t * half : (t + 1) * half]))
+        comm(j)
+        total = dr[...]
+        for t in range(2):
+            total = total + mm_nt(dv[:, t * half : (t + 1) * half], w(t, slice(0, half)))
+        dr[...] = total
+        advance()
+        term(layer, 1, jnp.sum(dv[...].astype(F32), axis=0, keepdims=True))
+        fetch(j + 2)
+        if layer == 1:
+            load(0, "o", "x")
+
+    def score_stage(layer, j):
+        probs, q, k, v = (bufs[i] for i in ("probs", "q", "k", "v"))
+        w = weights(j)
+        need("q", "k", "v")
+        kt[...] = k[...].T
+
+        def pair(p):
+            dop = d_o[:, block(p, 128)]
+            qp = q[:, block(p, 128)]
+            vp = v[:, block(p, 128)]
+            total = None
+            for head in range(2):
+                dp = mm_nt(vp, of_head(head, dop))
+                pr = probs[2 * p + head].astype(F32)
+                delta = jnp.sum(pr * dp, axis=0, keepdims=True)
+                ds = (pr * (dp - delta)).astype(BF)
+                r = mm(ds, of_head(head, qp))
+                total = r if total is None else total + r
+                rows = block(2 * p + head, HEAD)
+                dqt[rows, :] = (mm(kt[rows, :], ds) * (HEAD**-0.5)).astype(BF)
+            dk[:, block(p, 128)] = total.astype(BF)
+
+        def stage_cols(cut, n):
+            for t in range(2):
+                here = slice(t * half + cut * n, t * half + (cut + 1) * n)
+                put(j, t, slice(cut * n, (cut + 1) * n), mm(lot[...], dq[:, here]))
+                put(j, t, slice(half + cut * n, half + (cut + 1) * n), mm(lot[...], dk[:, here]))
+
+        if j < LAST:
+            for i in range(0, width // 128, 2):
+                pl.loop(i, i + 2)(pair)
+                advance()
+            dq[...] = dqt[...].T
+            stage_cols(0, half)
+            comm(j)
+        else:
+            n = half // CUTS
+            for cut in range(CUTS):
+
+                @pl.loop(0, 2)
+                def _(t):
+                    p = t * CUTS + cut
+                    pair(p)
+                    dq[:, block(p, n)] = dqt[block(p, n), :].T
+
+                stage_cols(cut, n)
+                comm(j, cut)
+        total = dr[...]
+        for t in range(2):
+            here = slice(t * half, (t + 1) * half)
+            total = total + mm_nt(dq[:, here], w(t, slice(0, half)))
+            total = total + mm_nt(dk[:, here], w(t, slice(half, width)))
+        term(layer, 0, jnp.sum(dq[...].astype(F32), axis=0, keepdims=True))
+        fetch(j + 2)
+        if layer == 1:
+            dy[...] = total
+            load(0, "probs", "q", "k", "v")
+        else:
+            d_input[...] = total
+
+    inside = lax.broadcasted_iota(jnp.int32, (n, 1), 0) < lengths[lax.axis_index("tensor")]
+    dy[...] = jnp.where(inside, grad[...].astype(F32), 0.0)
+    for j, wave in enumerate(ORDER):
+        layer, i = wave // 6, wave % 6
+        if i >= 4:
+            down_stage(layer, j, i - 4)
+        elif i >= 2:
+            up_stage(layer, j, i - 2)
+        elif i == 1:
+            value_stage(layer, j)
+        else:
+            score_stage(layer, j)
+    sums = sum_steps(terms, small_out, got, acc, (s_send, s_recv))
+    sums.pop(0)()
+    while moving or sums:
+        advance()
+        if sums:
+            sums.pop(0)()
+
+
+def back_all(lengths, grad, full, small, saved):
+    n, width = grad.shape
+    heads = width // HEAD
+    waves, _, _, _, _, part, cols = full.shape
+    kinds = saved_kinds(n, width)
     dma = pltpu.SemaphoreType.DMA
-    any_spec = pl.BlockSpec(memory_space=pl.ANY)
+    hbm = pl.BlockSpec(memory_space=pltpu.MemorySpace.HBM)
     vmem = pl.BlockSpec(memory_space=pltpu.VMEM)
+    shape = jax.ShapeDtypeStruct
+    rows = (n, width)
     return pl.pallas_call(
-        reduce_kernel,
-        out_shape=(
-            jax.ShapeDtypeStruct((WAVES, rows, cols), F32),
-            jax.ShapeDtypeStruct(small.shape, F32),
-        ),
-        in_specs=[any_spec] * WAVES + [vmem],
-        out_specs=(vmem, vmem),
-        scratch_shapes=[
-            pltpu.VMEM((2, NX, NZ, NY, rows, cols), BF),
-            pltpu.VMEM((WAVES, NX, NZ, NY, rows, cols), BF),
-            pltpu.VMEM((WAVES, NZ, NY, rows, cols // 2), BF),
-            pltpu.VMEM((WAVES, NX, NZ, rows, cols // 2), BF),
-            pltpu.VMEM((WAVES, NZ, rows, cols // 2), BF),
-            pltpu.VMEM((WAVES, NZ, rows, cols // 2), BF),
-            pltpu.VMEM((WAVES, 3, rows, cols), BF),
+        back_kernel,
+        out_shape=(shape(rows, F32), shape((waves, part, cols), F32), shape(small.shape, F32)),
+        in_specs=[pl.BlockSpec(memory_space=pltpu.SMEM), vmem, vmem, hbm] + [hbm] * 26,
+        out_specs=(vmem, vmem, vmem),
+        scratch_shapes=[pltpu.VMEM(*kinds[name]) for name in SAVED]
+        + [
+            pltpu.VMEM(rows, F32),
+            pltpu.VMEM(rows, F32),
+            pltpu.VMEM(rows, BF),
+            pltpu.VMEM((width, n), BF),
+            pltpu.VMEM((width, n), BF),
+            pltpu.VMEM(rows, BF),
+            pltpu.VMEM(rows, BF),
+            pltpu.VMEM(rows, BF),
+            pltpu.VMEM(rows, BF),
+            pltpu.VMEM((width, n), BF),
+            pltpu.VMEM((width, n), BF),
+            pltpu.VMEM((2, NX, NZ, NY, NC, part, cols), BF),
+            pltpu.VMEM((2, NX, NZ, NY, NC, part, cols), BF),
+            pltpu.VMEM((RC + 1, NX, NZ, NY, part, cols), BF),
+            pltpu.VMEM((R2S, NZ, NY, part, cols // 2), BF),
+            pltpu.VMEM((R2S, NX, NZ, part, cols // 2), BF),
+            pltpu.VMEM((R3S, NZ, part, cols // 2), BF),
+            pltpu.VMEM((R3S, NZ, part, cols // 2), BF),
+            pltpu.VMEM((waves, 3, part, cols), BF),
+            pltpu.VMEM((3, NX, NY, part, cols), BF),
+            pltpu.VMEM((3, part, cols // 2), BF),
+            pltpu.VMEM((3, part, cols // 2), BF),
+            pltpu.VMEM(small.shape, F32),
             pltpu.VMEM((6,) + small.shape, F32),
             pltpu.VMEM((3,) + small.shape, F32),
             dma((6,)),
             dma((6,)),
+            dma((waves + CUTS, 12)),
+            dma((waves + CUTS, 12)),
+            dma((8,)),
+            dma((8,)),
+            pltpu.SemaphoreType.REGULAR((5,)),
+            dma((13,)),
             dma((2,)),
-            dma((WAVES, 8)),
-            dma((WAVES, 8)),
         ],
-        name="reduce_all",
+        name="back_all",
         compiler_params=pltpu.CompilerParams(
-            collective_id=1, has_side_effects=True, vmem_limit_bytes=56 << 20
+            collective_id=1, has_side_effects=True, vmem_limit_bytes=63 << 20
         ),
-    )(*shaped, small)
+    )(lengths, grad, small, full, *[saved[i][name] for i in range(2) for name in SAVED])
+
+
+def unpack_kernel(*refs):
+    sums, small, d_input, activations = refs[:4]
+    act_out, d_out = refs[4:6]
+    outs = [refs[6 + 15 * i : 21 + 15 * i] for i in range(2)]
+    vectors, sem = refs[36:]
+    width = sums.shape[2]
+    half = width // 2
+    moves = [(small, vectors), (d_input, d_out), (activations, act_out)]
+    for layer in range(2):
+        wq, _, wk, wv, _, wo, _, _, _, wu, _, wd = outs[layer][:12]
+        at = 6 * layer
+        moves += [
+            (sums.at[at + 2], wu.at[:, :width]),
+            (sums.at[at + 3], wu.at[:, width:]),
+            (sums.at[at + 4], wd.at[:, :width]),
+            (sums.at[at + 5], wd.at[:, width:]),
+            (sums.at[at, :, :half], wq),
+            (sums.at[at, :, half:], wk),
+            (sums.at[at + 1, :, :half], wv),
+            (sums.at[at + 1, :, half:], wo),
+        ]
+    copies = [pltpu.make_async_copy(src, dst, sem.at[i]) for i, (src, dst) in enumerate(moves)]
+    for copy in copies:
+        copy.start()
+    dp, t, n_dp = lax.axis_index("dp"), lax.axis_index("tensor"), lax.axis_size("dp")
+    few, many = outs[0][1].shape[1], outs[0][10].shape[1]
+    from_norm = one_hot(width, few, (2 * dp + t) * few, 0)
+    from_bias = one_hot(width, few, (t * n_dp + dp) * few, 0)
+    from_up = [one_hot(width, many, (t * n_dp + dp) * many - i * width, 0) for i in range(4)]
+    copies[0].wait()
+    biases = mm_exact(vectors[...], from_bias)
+    norms = mm_exact(vectors[...], from_norm)
+    for layer in range(2):
+        _, bq, _, _, bv, _, bo, g1, s1, _, bu, _, bd, g2, s2 = outs[layer]
+        low = 12 * layer
+        for i, ref in enumerate((bq, bv)):
+            ref[...] = biases[low + i : low + i + 1]
+        for i, ref in enumerate((bo, g1, s1, bd, g2, s2)):
+            ref[...] = norms[low + 2 + i : low + 3 + i]
+    rows = [jnp.concatenate([vectors[8 + i : 9 + i, :], vectors[20 + i : 21 + i, :]], axis=0) for i in range(4)]
+    total = mm_exact(rows[0], from_up[0])
+    for i in range(1, 4):
+        total = total + mm_exact(rows[i], from_up[i])
+    for layer in range(2):
+        outs[layer][10][...] = total[layer : layer + 1]
+    for copy in copies[1:]:
+        copy.wait()
+
+
+def unpack_all(sums, small_sums, d_input, activations, teacher, student):
+    hbm = pl.BlockSpec(memory_space=pltpu.MemorySpace.HBM)
+    vmem = pl.BlockSpec(memory_space=pltpu.VMEM)
+    shape = jax.ShapeDtypeStruct
+    flat = teacher + student
+    outs = pl.pallas_call(
+        unpack_kernel,
+        out_shape=(shape(activations.shape, BF), shape(d_input.shape, F32))
+        + tuple(shape(v.shape, F32) for v in flat),
+        in_specs=[hbm] * 4,
+        out_specs=(vmem,) * 32,
+        scratch_shapes=[pltpu.VMEM(small_sums.shape, F32), pltpu.SemaphoreType.DMA((19,))],
+        name="unpack_all",
+        compiler_params=pltpu.CompilerParams(vmem_limit_bytes=63 << 20),
+    )(sums, small_sums, d_input, activations)
+    return outs[:2], outs[2:]
+
+
+def flat_params(args):
+    out = [v.reshape(1, -1) if v.ndim == 1 else v for v in args]
+    for i in (5, 11):
+        out[i] = out[i].T
+    return tuple(out)
+
+
+def shaped_grads(outs, args):
+    out = list(outs)
+    for i in (5, 11):
+        out[i] = out[i].T
+    return tuple(o.reshape(v.shape) for o, v in zip(out, args))
+
+
+def local_fast(n_dp, *args):
+    inputs, lengths, grad_out = args[0], args[1], args[-1]
+    teacher, student = args[2:17], args[17:32]
+    first, second = flat_params(teacher), flat_params(student)
+    full, small, activations, saved = forward_all(lengths, inputs, first, second)
+    d_input, sums, small_sums = back_all(lengths, grad_out, full, small, saved)
+    (activations, d_input), grads = unpack_all(sums, small_sums, d_input, activations, first, second)
+    return (activations, d_input) + shaped_grads(grads[:15], teacher) + shaped_grads(grads[15:], student)
 
 
 def gather_plain(shard, small):
@@ -414,7 +1260,7 @@
     return lax.dynamic_slice_in_dim(values, where * m, m, 1)
 
 
-def local(n_dp, fast, *args):
+def local_plain(n_dp, *args):
     inputs, lengths, grad_out = args[0], args[1], args[-1]
     teacher, student = args[2:17], args[17:32]
     dp, t = lax.axis_index("dp"), lax.axis_index("tensor")
@@ -427,7 +1273,7 @@
     valid = inside[None, None, None, :]
     shard = jnp.concatenate([pack_weights(teacher), pack_weights(student)], axis=0)
     small = jnp.concatenate([pack_small(teacher, dp, n_dp, t), pack_small(student, dp, n_dp, t)], axis=0)
-    full, small = (gather_all if fast else gather_plain)(shard, small)
+    full, small = gather_plain(shard, small)
     groups = [tuple(full[3 * layer + i] for i in range(3)) for layer in range(2)]
     smalls = [small[:12], small[12:]]
     result, kept_t = layer_forward(inputs, groups[0], smalls[0], valid)
@@ -437,7 +1283,7 @@
     d_current, parts_s, small_s = layer_backward(d_current, groups[1], smalls[1], kept_s, valid)
     d_current, parts_t, small_t = layer_backward(d_current, groups[0], smalls[0], kept_t, valid)
     order = (parts_s[2], parts_s[1], parts_s[0], parts_t[2], parts_t[1], parts_t[0])
-    sums, small_sums = (reduce_all if fast else reduce_plain)(order, jnp.concatenate([small_t, small_s], axis=0))
+    sums, small_sums = reduce_plain(order, jnp.concatenate([small_t, small_s], axis=0))
     outs = [activations, d_current]
     for layer in range(2):
         base = 3 * (1 - layer)
@@ -474,7 +1320,7 @@
     cut_in, cut_out = P("dp", "tensor"), P("tensor", "dp")
     layer = (cut_in, cut_out, cut_in, cut_in, cut_out, cut_out, vec, vec, vec, cut_in, cut_out, cut_out, vec, vec, vec)
     return jax.shard_map(
-        functools.partial(local, n_dp, fast),
+        functools.partial(local_fast if fast else local_plain, n_dp),
         mesh=mesh,
         in_specs=(row, P("dp")) + layer + layer + (row,),
         out_specs=(row, row) + layer + layer,

time: 629 us -> 318 us (0.51)
  matrix products: 186 us -> 0 us
  local copies, waits for them, and re-layouts: 75.3 us -> 0 us
  other arithmetic: 41.8 us -> 0 us
    dot_general x36 -> x0, matrix products: 186 us -> none  [ein(): return jnp.einsum(spec, a, b, preferred_element_type=F32)]
    slice x9 -> x0, local copies, waits for them, and re-layouts: 24.5 us -> none  [the longest x1 21.1 us: local(): full[3 * layer + i]]
    reshape x20 -> x0, local copies, waits for them, and re-layouts: 17.9 us -> none  [the longest x2 4.61 us: layer_backward(): ein('thqk,tqhd->tkhd', probs.astype(BF), heads_of(d_attended)).astype(BF)]
    convert_element_type x6 -> x0, other arithmetic: 16.9 us -> none  [the longest x2 14.1 us: layer_backward(): (probs * (d_probs - jnp.sum(probs * d_probs, axis=-1, keepdims=True))).as...]
    reduce_sum x15 -> x0, other arithmetic: 12.1 us -> none  [the longest x4 5.75 us: layer_norm(): centred = residual - average]
    unnamed x150 -> x0, local copies, waits for them, and re-layouts: 11.5 us -> none
    transpose x5 -> x0, local copies, waits for them, and re-layouts: 7.97 us -> none  [the longest x2 4.07 us: ein(): return jnp.einsum(spec, a, b, preferred_element_type=F32)]
    concatenate x2 -> x0, other arithmetic: 7.7 us -> none  [layer_backward(): jnp.concatenate([ein('nd,tnc->tdc', rows, d_qkv), gw_out], axis=2)]
where the time goes in v2:
time: 318 us; the launch traced here: 315 us
  Pallas kernels  314 us (99%)
    pallas_call x1, Pallas kernels, back_all(): pl.pallas_call(back_kernel, out_shape=(shape(rows, F32), shape((waves, pa...  157 us
    pallas_call x1, Pallas kernels, forward_all(): pl.pallas_call(forward_kernel, out_shape=(shape((waves, NX, NZ, NY, NC, p...  153 us

profile of v2, /device:TPU:0, one launch (start us, length us, event | category | flops | bytes accessed | tf_op | source)
XLA Modules:
  0.0 315.3 jit_solution(15694041611749571196)
XLA Ops:
  0.7 152.7 %forward_all.1 = (bf16[12,2,4,2,2,48,768]{6,5,4,3,2,1,0:T(8,128)(2,1)}, f32[24,768]{1,0:T(8,128)}, bf16[512,768]{1,0:T(8,128)(2,1)}, bf16[512,768]{1,0:T(8,128)(...) custom-call(s32[2]{0:T(128)} %refs_0_.3, ...), custom_call_target="tpu_custom_call" | custom-call | tf_op jit(solution)/shard_map/forward_all/pallas_call | solution.py:510
  153.4 157.3 %back_all.1 = (f32[512,768]{1,0:T(8,128)}, f32[12,48,768]{2,1,0:T(8,128)}, f32[24,768]{1,0:T(8,128)}) custom-call(s32[2]{0:T(128)} %refs_0_.3, bf16[512,768]{1,0:T(8,128)(2,1)} %refs_1_.3, f32[24,768]{1,0:T(8,128)} %get-tuple-element.96.refs_2_, bf16[12,2,4,2,2,48,768]{6,5,4,3,2,1,0:T(8,128)(2,1)} %get-tuple-element.97.refs_3_, ...), custom_call_target="tpu_custom_call" | custom-call | tf_op jit(solution)/shard_map/back_all/pallas_call | solution.py:984
  310.6 4.4 %unpack_all.1 = (bf16[512,768]{1,0:T(8,128)(2,1)}, f32[512,768]{1,0:T(8,128)}, f32[48,384]{1,0:T(8,128)}, f32[1,24]{1,0:T(1,128)}, f32[48,384]{1,0:T(8,128)}, /*...) custom-call(f32[12,48,768]{2,1,0:T(8,128)} %get-tuple-element.124.re, ...), custom_call_target="tpu_custom_call" | custom-call | tf_op jit(solution)/shard_map/unpack_all/pallas_call | solution.py:1087

commit v3 on v2

--- a/solution.py
+++ b/solution.py
@@ -102,6 +102,7 @@
 
 FWAVES = 12
 AHEAD = 2
+BULK = (5, 7, 9, 10)
 SIDE = FWAVES - 1
 
 
@@ -331,15 +332,15 @@
             two(step)
             if step + AHEAD < SIDE:
                 one(step + AHEAD)
-        if step % 2 == 1 and step < 8:
-            side[2](step // 2)
+        if step in BULK:
+            side[2](BULK.index(step))
         if 0 <= step - 1 < SIDE:
             three(step - 1)
-        if step == SIDE - 1:
+        if step == SIDE:
             side[3]()
         if 0 <= step - 2 < SIDE:
             four(step - 2)
-        if 0 <= step - 3 < FWAVES:
+        if 0 <= step - 3 < SIDE - 1:
             bring(step - 3)
 
     def weights(k):
@@ -443,7 +444,7 @@
         for t in range(2):
             r = mm_nt(g[t, :, here], w(t, slice(0, width)))
             total = r if total is None else total + r
-        if part == 0:
+        if part == layer:
             r2[...] = total
             return
         free("z2", "rstd2", "x")
@@ -469,10 +470,13 @@
         else:
             down_stage(layer, k, i - 4)
 
-    for step in range(FWAVES + 4):
+    for step in range(SIDE + 3):
         comm(step)
         if step >= 4:
             compute(step - 4)
+    for k in (SIDE, SIDE - 1):
+        bring(k)
+        compute(k)
     free(*list(stores))
 
 
@@ -721,7 +725,7 @@
 
         return [one, two] + [rest] * RESTS + [three, rest, rest, four, rest, rest, five]
 
-    return steps, turned
+    return steps, turned, rest
 
 
 def back_kernel(*refs):
@@ -768,7 +772,7 @@
     fetch(1)
     load(1, "o", "probs", "x", "v", "k", "q")
     greet([core, over_x, over_y] + over_z)
-    steps, turned = reduce_steps(
+    steps, turned, rest = reduce_steps(
         stage, rc, r2a, r2b, r3a, r3b, r4, rz, ra, rb, out, credit, (b_send, b_recv), (t_send, t_recv)
     )
     moving = []
@@ -965,10 +969,15 @@
             score_stage(layer, j)
     sums = sum_steps(terms, small_out, got, acc, (s_send, s_recv))
     sums.pop(0)()
-    while moving or sums:
-        advance()
+    moving = [[step for step in item if step is not rest] for item in moving]
+    while any(len(item) > 1 for item in moving):
+        for item in moving:
+            if len(item) > 1:
+                item.pop(0)()
         if sums:
             sums.pop(0)()
+    for step in [item[0] for item in moving] + sums:
+        step()
 
 
 def back_all(lengths, grad, full, small, saved):

time: 318 us -> 306 us (0.962)
  Pallas kernels: 314 us -> 302 us
    pallas_call x1, Pallas kernels: 157 us -> 147 us  [back_all(): pl.pallas_call(back_kernel, out_shape=(shape(rows, F32), shape((waves, pa...]
where the time goes in v3:
time: 306 us; the launch traced here: 303 us
  Pallas kernels  302 us (99%)
    pallas_call x1, Pallas kernels, forward_all(): pl.pallas_call(forward_kernel, out_shape=(shape((waves, NX, NZ, NY, NC, p...  150 us
    pallas_call x1, Pallas kernels, back_all(): pl.pallas_call(back_kernel, out_shape=(shape(rows, F32), shape((waves, pa...  147 us

profile of v3, /device:TPU:0, one launch (start us, length us, event | category | flops | bytes accessed | tf_op | source)
XLA Modules:
  0.0 302.6 jit_solution(9501906800443785891)
XLA Ops:
  0.7 149.8 %forward_all.1 = (bf16[12,2,4,2,2,48,768]{6,5,4,3,2,1,0:T(8,128)(2,1)}, f32[24,768]{1,0:T(8,128)}, bf16[512,768]{1,0:T(8,128)(2,1)}, bf16[512,768]{1,0:T(8,128)(...) custom-call(s32[2]{0:T(128)} %refs_0_.3, ...), custom_call_target="tpu_custom_call" | custom-call | tf_op jit(solution)/shard_map/forward_all/pallas_call | solution.py:514
  150.5 147.4 %back_all.1 = (f32[512,768]{1,0:T(8,128)}, f32[12,48,768]{2,1,0:T(8,128)}, f32[24,768]{1,0:T(8,128)}) custom-call(s32[2]{0:T(128)} %refs_0_.3, bf16[512,768]{1,0:T(8,128)(2,1)} %refs_1_.3, f32[24,768]{1,0:T(8,128)} %get-tuple-element.96.refs_2_, bf16[12,2,4,2,2,48,768]{6,5,4,3,2,1,0:T(8,128)(2,1)} %get-tuple-element.97.refs_3_, ...), custom_call_target="tpu_custom_call" | custom-call | tf_op jit(solution)/shard_map/back_all/pallas_call | solution.py:993
  297.9 4.4 %unpack_all.1 = (bf16[512,768]{1,0:T(8,128)(2,1)}, f32[512,768]{1,0:T(8,128)}, f32[48,384]{1,0:T(8,128)}, f32[1,24]{1,0:T(1,128)}, f32[48,384]{1,0:T(8,128)}, /*...) custom-call(f32[12,48,768]{2,1,0:T(8,128)} %get-tuple-element.124.re, ...), custom_call_target="tpu_custom_call" | custom-call | tf_op jit(solution)/shard_map/unpack_all/pallas_call | solution.py:1096

commit v4 on v3

--- a/solution.py
+++ b/solution.py
@@ -31,7 +31,7 @@
     barrier = pltpu.get_barrier_semaphore()
     for other in others:
         pl.semaphore_signal(barrier, inc=1, device_id=other, device_id_type=MESH)
-    pl.semaphore_wait(barrier, len(others))
+    return lambda: pl.semaphore_wait(barrier, len(others))
 
 
 def send(src, dst, sems, index, other):
@@ -282,6 +282,7 @@
     z, y, c, t_mine = place()
     dp = lax.axis_index("dp")
     core, over_x, over_y, over_z = partners()
+    arrived = greet([core, over_x, over_y] + over_z)
     pieces = pack_copies(raw, shard, r_bias, r_up, r_norm, raw_sem)
     x_copy = pltpu.make_async_copy(rows, bufs["x"], x_sem)
     for name in ("qk0", "d1", "small", "vo0", "u0", "d0", "qk1", "vo1", "u1"):
@@ -289,7 +290,7 @@
             copy.start()
         if name == "vo0":
             x_copy.start()
-    greet([core, over_x, over_y] + over_z)
+    arrived()
     one, two, three, four, five, side = gather_steps(
         shard, full, own_sem, (b_send, b_recv), (c_send, c_recv)
     )
@@ -766,12 +767,12 @@
         slot = w_slots.at[j % 2]
         return lambda t, lanes: slot[t, :, :, :, :, lanes].reshape(width, -1)
 
+    arrived = greet([core, over_x, over_y] + over_z)
     load(1, "z2", "rstd2")
     fetch(0)
     load(1, "g", "gp", "h", "z1", "rstd1")
     fetch(1)
     load(1, "o", "probs", "x", "v", "k", "q")
-    greet([core, over_x, over_y] + over_z)
     steps, turned, rest = reduce_steps(
         stage, rc, r2a, r2b, r3a, r3b, r4, rz, ra, rb, out, credit, (b_send, b_recv), (t_send, t_recv)
     )
@@ -817,6 +818,8 @@
             need("z2", "rstd2")
             norm_back(layer, 5, dy[...], bufs["z2"], bufs["rstd2"])
             need("g", "gp")
+            if j == 0:
+                arrived()
         w = weights(j)
         here = slice(part * width, (part + 1) * width)
         for t in range(2):

time: 306 us -> 306 us (level)
  no operation moved by 1% of the time
where the time goes in v4:
time: 306 us; the launch traced here: 303 us
  Pallas kernels  302 us (99%)
    pallas_call x1, Pallas kernels, forward_all(): pl.pallas_call(forward_kernel, out_shape=(shape((waves, NX, NZ, NY, NC, p...  150 us
    pallas_call x1, Pallas kernels, back_all(): pl.pallas_call(back_kernel, out_shape=(shape(rows, F32), shape((waves, pa...  147 us

profile of v4, /device:TPU:0, one launch (start us, length us, event | category | flops | bytes accessed | tf_op | source)
XLA Modules:
  0.0 302.6 jit_solution(407505820484896944)
XLA Ops:
  0.7 149.8 %forward_all.1 = (bf16[12,2,4,2,2,48,768]{6,5,4,3,2,1,0:T(8,128)(2,1)}, f32[24,768]{1,0:T(8,128)}, bf16[512,768]{1,0:T(8,128)(2,1)}, bf16[512,768]{1,0:T(8,128)(...) custom-call(s32[2]{0:T(128)} %refs_0_.3, ...), custom_call_target="tpu_custom_call" | custom-call | tf_op jit(solution)/shard_map/forward_all/pallas_call | solution.py:515
  150.4 147.4 %back_all.1 = (f32[512,768]{1,0:T(8,128)}, f32[12,48,768]{2,1,0:T(8,128)}, f32[24,768]{1,0:T(8,128)}) custom-call(s32[2]{0:T(128)} %refs_0_.3, bf16[512,768]{1,0:T(8,128)(2,1)} %refs_1_.3, f32[24,768]{1,0:T(8,128)} %get-tuple-element.96.refs_2_, bf16[12,2,4,2,2,48,768]{6,5,4,3,2,1,0:T(8,128)(2,1)} %get-tuple-element.97.refs_3_, ...), custom_call_target="tpu_custom_call" | custom-call | tf_op jit(solution)/shard_map/back_all/pallas_call | solution.py:996
  297.9 4.4 %unpack_all.1 = (bf16[512,768]{1,0:T(8,128)(2,1)}, f32[512,768]{1,0:T(8,128)}, f32[48,384]{1,0:T(8,128)}, f32[1,24]{1,0:T(1,128)}, f32[48,384]{1,0:T(8,128)}, /*...) custom-call(f32[12,48,768]{2,1,0:T(8,128)} %get-tuple-element.124.re, ...), custom_call_target="tpu_custom_call" | custom-call | tf_op jit(solution)/shard_map/unpack_all/pallas_call | solution.py:1099
